TPU v7x, 512 devices: a whole 4x8x8 slice. The times are simulated.
512 devices in a mesh: row: 16 (over z, y_hi), col: 32 (over y_lo, x, core).
Axes of the slice: x: 4, y: 8 (y_hi: 2, y_lo: 4; y = y_hi * 4 + y_lo), z: 8, core: 2. Of those that a mesh axis runs over, the one named last changes fastest.
Arguments:
- grid_input: bfloat16 [256, 256, 1024], P('row', 'col'), may hold values from -6 to 6
- w_qkv: bfloat16 [1024, 1536], replicated, may hold values from -0.1875 to 0.1875
- out_weight: bfloat16 [1024, 512], replicated, may hold values from -0.25 to 0.25
- head_scale: float32 [8], replicated, may hold values from 4 to 16
- cotangent: bfloat16 [256, 256, 1024], P('row', 'col'), may hold values from -16 to 16
Outputs:
- d_input: bfloat16 [256, 256, 1024], P('row', 'col')
All inputs are finite; a program needn't handle non-finite values.
Results may differ from a plain program's by a relative error of at most 0.012.
Values may be sent and summed in bfloat16 or wider, within the bound.
A program may use at most 64 MiB of HBM per device.

v0:
```python
import jax
import jax.numpy as jnp
from jax import lax
from jax.sharding import PartitionSpec as P

D = 1024
HEADS = 8
HEAD_DIM = 64
RADIUS = 8


norm_epsilon = 1e-06


def passed_along(value, axis, steps):
    count = lax.axis_size(axis)
    initial, last = (max(0, -steps), min(count, count - steps))
    return lax.ppermute(value, axis, [(source, source + steps) for source in range(initial, last)])


def extended(array, sides, width):
    for axis, dim in sides:
        size, length = (lax.axis_size(axis), array.shape[dim])
        up = [(i, (i + 1) % size) for i in range(size - 1)]
        down = [(j, i) for i, j in up]
        last = lax.slice_in_dim(array, length - width, length, axis=dim)
        initial = lax.slice_in_dim(array, 0, width, axis=dim)
        before = lax.ppermute(last, axis, up)
        after = lax.ppermute(initial, axis, down)
        array = jnp.concatenate([before, array, after], axis=dim)
    return array


def unit_heads(raw_heads, head_scale):
    shaped = raw_heads.reshape(raw_heads.shape[:-1] + (HEADS, HEAD_DIM))
    squares = jnp.sum(shaped * shaped, axis=-1, keepdims=True) + norm_epsilon
    scaled = shaped * jnp.sqrt(head_scale)[:, None] * lax.rsqrt(squares)
    return scaled.reshape(raw_heads.shape)


def unit_heads_back(raw_heads, upstream, head_scale):
    shaped = raw_heads.reshape(raw_heads.shape[:-1] + (HEADS, HEAD_DIM))
    grads = upstream.reshape(shaped.shape)
    squares = jnp.sum(shaped * shaped, axis=-1, keepdims=True) + norm_epsilon
    along_raw = jnp.sum(grads * shaped, axis=-1, keepdims=True) / squares
    result = jnp.sqrt(head_scale)[:, None] * lax.rsqrt(squares) * (grads - shaped * along_raw)
    return result.reshape(raw_heads.shape)


def pair_window(first, second, extent):
    near_enough = jnp.abs(first[:, None] - second[None, :]) <= RADIUS
    inside = (
        (first[:, None] >= 0)
        & (first[:, None] < extent)
        & (second[None, :] >= 0)
        & (second[None, :] < extent)
    )
    return near_enough & inside


def window_mask(query_rows, query_cols, key_rows, key_cols, height, width_grid):
    rows_ok = pair_window(query_rows, key_rows, height)
    cols_ok = pair_window(query_cols, key_cols, width_grid)
    joined = rows_ok[:, None, :, None] & cols_ok[None, :, None, :]
    return joined.reshape(
        query_rows.shape[0] * query_cols.shape[0], key_rows.shape[0] * key_cols.shape[0]
    )


def head_view(array):
    return array.reshape(array.shape[0], HEADS, HEAD_DIM)


def key_terms(dscore, probs_bf, queries, cotangents):
    dkey = jnp.einsum(
        "hqk,qhd->khd", dscore, head_view(queries), preferred_element_type=jnp.float32
    )
    dvalue = jnp.einsum(
        "hqk,qhd->khd", probs_bf, head_view(cotangents), preferred_element_type=jnp.float32
    )
    count_k = dkey.shape[0]
    return jnp.concatenate([dkey.reshape(count_k, -1), dvalue.reshape(count_k, -1)], axis=-1)


def query_side(queries, cotangents, keys, values, window, head_scale):
    cot_heads = head_view(cotangents)
    value_heads = head_view(values)
    scores = jnp.einsum(
        "qhd,khd->hqk", head_view(queries), head_view(keys), preferred_element_type=jnp.float32
    )
    weights = jnp.where(window[None], jnp.exp(scores - head_scale[:, None, None]), 0.0)
    totals = jnp.sum(weights, axis=-1)
    probs = weights / totals[:, :, None]
    probs_bf = probs.astype(jnp.bfloat16)
    attended = jnp.einsum("hqk,khd->hqd", probs_bf, value_heads, preferred_element_type=jnp.float32)
    delta = jnp.sum(jnp.transpose(cot_heads, (1, 0, 2)).astype(jnp.float32) * attended, axis=-1)
    dprobs = jnp.einsum("qhd,khd->hqk", cot_heads, value_heads, preferred_element_type=jnp.float32)
    dscore = (probs * (dprobs - delta[:, :, None])).astype(jnp.bfloat16)
    dquery = jnp.einsum("hqk,khd->qhd", dscore, head_view(keys), preferred_element_type=jnp.float32)
    return (dquery.reshape(queries.shape[0], -1), dscore, probs_bf, totals, delta)


def pass_rows(piece, offset):
    return passed_along(piece.astype(jnp.bfloat16), "row", offset).astype(piece.dtype)


def pass_cols(piece, offset):
    return passed_along(piece.astype(jnp.bfloat16), "col", offset).astype(piece.dtype)


def return_rims(terms, tile_h, tile_w):
    from_below = pass_rows(terms[:RADIUS], -1)
    from_above = pass_rows(terms[tile_h + RADIUS :], 1)
    middle = terms[RADIUS : RADIUS + tile_h]
    middle = middle + jnp.pad(from_below, ((tile_h - RADIUS, 0), (0, 0), (0, 0)))
    middle = middle + jnp.pad(from_above, ((0, tile_h - RADIUS), (0, 0), (0, 0)))
    from_right = pass_cols(middle[:, :RADIUS], -1)
    from_left = pass_cols(middle[:, tile_w + RADIUS :], 1)
    centre = middle[:, RADIUS : RADIUS + tile_w]
    centre = centre + from_right
    centre = centre + from_left
    return centre


def per_device(grid_input, w_qkv, out_weight, head_scale, cotangent):
    tile_h, tile_w = (grid_input.shape[0], grid_input.shape[1])
    width_heads = out_weight.shape[1]
    height = tile_h * lax.axis_size("row")
    width_grid = tile_w * lax.axis_size("col")
    span_h = tile_h + 2 * RADIUS
    span_w = tile_w + 2 * RADIUS
    row_start = lax.axis_index("row") * tile_h
    col_start = lax.axis_index("col") * tile_w
    own_rows = row_start + jnp.arange(tile_h, dtype=jnp.int32)
    own_cols = col_start + jnp.arange(tile_w, dtype=jnp.int32)
    near_rows = row_start - RADIUS + jnp.arange(span_h, dtype=jnp.int32)
    near_cols = col_start - RADIUS + jnp.arange(span_w, dtype=jnp.int32)
    tokens = grid_input.reshape(-1, D)
    d_att = jnp.dot(
        cotangent.reshape(-1, D), out_weight, preferred_element_type=jnp.float32
    ).astype(jnp.bfloat16)
    projected = jnp.dot(tokens, w_qkv, preferred_element_type=jnp.float32)
    query_raw = projected[:, :width_heads]
    key_raw = projected[:, width_heads : 2 * width_heads]
    query_hat = unit_heads(query_raw, head_scale).astype(jnp.bfloat16)
    key_hat = unit_heads(key_raw, head_scale).astype(jnp.bfloat16)
    values = projected[:, 2 * width_heads :].astype(jnp.bfloat16)
    outgoing = jnp.concatenate([key_hat, values], axis=-1)
    arrived = extended(outgoing.reshape(tile_h, tile_w, -1), (("row", 0), ("col", 1)), RADIUS)
    arrived = arrived.reshape(span_h * span_w, -1)
    near_keys = arrived[:, :width_heads]
    near_values = arrived[:, width_heads : 2 * width_heads]
    own_window = window_mask(own_rows, own_cols, near_rows, near_cols, height, width_grid)
    dquery_hat, dscore, probs_bf, totals, delta = query_side(
        query_hat, d_att, near_keys, near_values, own_window, head_scale
    )
    terms = key_terms(dscore, probs_bf, query_hat, d_att).reshape(span_h, span_w, 2 * width_heads)
    key_grads = return_rims(terms, tile_h, tile_w).reshape(-1, 2 * width_heads)
    dquery = unit_heads_back(query_raw, dquery_hat, head_scale)
    dkey = unit_heads_back(key_raw, key_grads[:, :width_heads], head_scale)
    dqkv = jnp.concatenate([dquery, dkey, key_grads[:, width_heads:]], axis=-1).astype(jnp.bfloat16)
    d_input = jnp.einsum("nf,df->nd", dqkv, w_qkv, preferred_element_type=jnp.float32).astype(
        jnp.bfloat16
    )
    return d_input.reshape(tile_h, tile_w, D)


def solution(mesh):
    placed = (P("row", "col", None), P(), P(), P(), P("row", "col", None))
    return jax.shard_map(
        per_device, mesh=mesh, in_specs=placed, out_specs=P("row", "col", None), check_vma=False
    )
```

profile of v0, /device:TPU:168, one launch (start us, length us, event | category | flops | bytes accessed | tf_op | source)
XLA Modules:
  0.0 150.3 jit_solution(8269698298297228720)
XLA Ops:
  13.8 1.9 %multiply_convert_fusion.4 = (bf16[128,512]{1,0:T(8,128)(2,1)S(1)}, bf16[128,512]{1,0:T(8,128)(2,1)}) fusion(f32[128,512]{1,0:T(8,128)} %copy.25, f32[128,1536]{1,0:T(8,128)} %copy-done.2, f32[512]{0:T(512)S(1)} %mul.141, f32[128,512]{1,0:T(8,128)} %copy.27), kind=kLoop, calls=%fused_computation.47 | loop fusion | flops 393216 | bytes 1312768 | tf_op jit(solution)/shard_map/convert_element_type | solution.py:146
  17.3 4.7 %collective-permute-start = (bf16[8,8,1024]{2,1,0:T(8,128)(2,1)}, bf16[8,8,1024]{2,1,0:T(8,128)(2,1)}, u32[]{:S(2)}, u32[]{:S(2)}) collective-permute-start(bf16[8,8,1024]{2,1,0:T(8,128)(2,1)} %get-tuple-element.17), channel_id=1, source_target_pairs={{0,32},{32,64},{64,96},{96,128},{128,160},{160,192},{192,224},{224... | collective-permute-start | bytes 393224 | tf_op jit(solution)/shard_map/ppermute | solution.py:28
  22.0 5.0 %collective-permute-start.1 = (bf16[8,8,1024]{2,1,0:T(8,128)(2,1)}, bf16[8,8,1024]{2,1,0:T(8,128)(2,1)}, u32[]{:S(2)}, u32[]{:S(2)}) collective-permute-start(bf16[8,8,1024]{2,1,0:T(8,128)(2,1)} %get-tuple-element.18), channel_id=1, source_target_pairs={{32,0},{64,32},{96,64},{128,96},{160,128},{192,160},{224,192},{256... | collective-permute-start | bytes 393224 | tf_op jit(solution)/shard_map/ppermute | solution.py:29
  29.9 2.3 %convolution_convert_fusion.1 = bf16[128,512]{1,0:T(8,128)(2,1)} fusion(bf16[1024,512]{1,0:T(8,128)(2,1)} %param.7, bf16[16,8,1024]{2,1,0:T(8,128)(2,1)} %param.9), kind=kOutput, calls=%fused_computation.15 | convolution fusion | flops 134283264 | bytes 1441792 | tf_op jit(solution)/shard_map/dot_general | solution.py:139
  36.0 3.0 %collective-permute-done.1 = bf16[8,8,1024]{2,1,0:T(8,128)(2,1)} collective-permute-done((bf16[8,8,1024]{2,1,0:T(8,128)(2,1)}, bf16[8,8,1024]{2,1,0:T(8,128)(2,1)}, u32[]{:S(2)}, u32[]{:S(2)}) %collective-permute-start.1) | collective-permute-done | bytes 131104 | tf_op jit(solution)/shard_map/ppermute | solution.py:29
  40.9 2.0 %collective-permute-start.3 = (bf16[32,8,1024]{2,1,0:T(8,128)(2,1)}, bf16[32,8,1024]{2,1,0:T(8,128)(2,1)}, u32[]{:S(2)}, u32[]{:S(2)}) collective-permute-start(bf16[32,8,1024]{2,1,0:T(8,128)(2,1)} %pad_maximum_fusion.2), channel_id=1, source_target_pairs={{1,0},{2,1},{3,2},{4,3},{5,4},{6,5},{7,6},{8,7},{9,8},{10,9},{11,1... | collective-permute-start | bytes 1572872 | tf_op jit(solution)/shard_map/ppermute | solution.py:29
  42.9 2.3 %collective-permute-start.2 = (bf16[32,8,1024]{2,1,0:T(8,128)(2,1)}, bf16[32,8,1024]{2,1,0:T(8,128)(2,1)}, u32[]{:S(2)}, u32[]{:S(2)}) collective-permute-start(bf16[32,8,1024]{2,1,0:T(8,128)(2,1)} %pad_maximum_fusion.2), channel_id=1, source_target_pairs={{0,1},{1,2},{2,3},{3,4},{4,5},{5,6},{6,7},{7,8},{8,9},{9,10},{10,1... | collective-permute-start | bytes 1572872 | tf_op jit(solution)/shard_map/ppermute | solution.py:28
  47.1 3.0 %and.127 = pred[128,768]{1,0:T(8,128)(4,1)} reshape(pred[16,8,32,24]{3,2,1,0:T(8,128)(4,1)} %broadcast_and_fusion) | data formatting | bytes 196608 | tf_op jit(solution)/shard_map/and | solution.py:64
  51.2 4.6 %collective-permute-done.2 = bf16[32,8,1024]{2,1,0:T(8,128)(2,1)} collective-permute-done((bf16[32,8,1024]{2,1,0:T(8,128)(2,1)}, bf16[32,8,1024]{2,1,0:T(8,128)(2,1)}, u32[]{:S(2)}, u32[]{:S(2)}) %collective-permute-start.2) | collective-permute-done | bytes 524320 | tf_op jit(solution)/shard_map/ppermute | solution.py:28
  58.6 2.3 %copy.39 = bf16[768,512]{0,1:T(8,128)(2,1)} copy(bf16[768,512]{1,0:T(8,128)(2,1)} %get-tuple-element.9) | data formatting | bytes 1572864
  60.9 2.3 %copy.38 = bf16[768,512]{0,1:T(8,128)(2,1)} copy(bf16[768,512]{1,0:T(8,128)(2,1)} %get-tuple-element.10) | data formatting | bytes 1572864
  63.2 2.2 %fusion.2 = (f32[8,128]{1,0:T(8,128)S(1)}, f32[8,128,768]{2,1,0:T(8,128)S(1)}) fusion(f32[8]{0:T(128)S(1)} %copy-done.15, pred[128,768]{1,0:T(8,128)(4,1)} %and.127, bf16[128,8,64]{0,2,1:T(8,128)(2,1)S(1)} %bitcast.76, bf16[768,8,64]{0,2,1:T(8,128)(2,1)} %bitcast.68), kind=kOutput, calls=%fused_computation.7 | convolution fusion | flops 103021568 | bytes 4165664 | tf_op jit(solution)/shard_map/qhd,khd->hqk/dot_general | solution.py:88
  72.0 2.0 %copy.32 = bf16[192,1024]{1,0:T(8,128)(2,1)} copy(bf16[192,1024]{0,1:T(8,128)(2,1)} %get-tuple-element.7) | data formatting | bytes 786432 | tf_op jit(solution)/shard_map/slice | solution.py:112
  74.0 2.0 %copy.33 = bf16[192,1024]{1,0:T(8,128)(2,1)} copy(bf16[192,1024]{0,1:T(8,128)(2,1)} %get-tuple-element.8) | data formatting | bytes 786432 | tf_op jit(solution)/shard_map/slice | solution.py:113
  76.0 5.3 %collective-permute-start.5 = (bf16[8,24,1024]{2,1,0:T(8,128)(2,1)}, bf16[8,24,1024]{2,1,0:T(8,128)(2,1)}, u32[]{:S(2)}, u32[]{:S(2)}) collective-permute-start(bf16[8,24,1024]{2,1,0:T(8,128)(2,1)} %bitcast.80), channel_id=1, source_target_pairs={{0,32},{32,64},{64,96},{96,128},{128,160},{160,192},{192,224},{224... | collective-permute-start | bytes 1179656 | tf_op jit(solution)/shard_map/ppermute | solution.py:18
  81.3 4.4 %collective-permute-start.4 = (bf16[8,24,1024]{2,1,0:T(8,128)(2,1)}, bf16[8,24,1024]{2,1,0:T(8,128)(2,1)}, u32[]{:S(2)}, u32[]{:S(2)}) collective-permute-start(bf16[8,24,1024]{2,1,0:T(8,128)(2,1)} %bitcast.79), channel_id=1, source_target_pairs={{32,0},{64,32},{96,64},{128,96},{160,128},{192,160},{224,192},{256... | collective-permute-start | bytes 1179656 | tf_op jit(solution)/shard_map/ppermute | solution.py:18
  85.8 3.2 %fusion.3 = f32[384,1024]{0,1:T(8,128)} fusion(f32[768,512]{0,1:T(8,128)} %bitcast.63, f32[768,512]{0,1:T(8,128)} %bitcast.67), kind=kLoop, calls=%fused_computation.8 | loop fusion | flops 393216 | bytes 4718592 | tf_op jit(solution)/shard_map/concatenate | solution.py:82
  89.0 3.0 %copy.31 = f32[384,1024]{1,0:T(8,128)} copy(f32[384,1024]{0,1:T(8,128)} %fusion.3) | data formatting | bytes 3145728 | tf_op jit(solution)/shard_map/slice | solution.py:114
  92.0 11.1 %collective-permute-done.5 = bf16[8,24,1024]{2,1,0:T(8,128)(2,1)} collective-permute-done((bf16[8,24,1024]{2,1,0:T(8,128)(2,1)}, bf16[8,24,1024]{2,1,0:T(8,128)(2,1)}, u32[]{:S(2)}, u32[]{:S(2)}) %collective-permute-start.5) | collective-permute-done | bytes 393248 | tf_op jit(solution)/shard_map/ppermute | solution.py:18
  103.1 9.0 %collective-permute-done.4 = bf16[8,24,1024]{2,1,0:T(8,128)(2,1)} collective-permute-done((bf16[8,24,1024]{2,1,0:T(8,128)(2,1)}, bf16[8,24,1024]{2,1,0:T(8,128)(2,1)}, u32[]{:S(2)}, u32[]{:S(2)}) %collective-permute-start.4) | collective-permute-done | bytes 393248 | tf_op jit(solution)/shard_map/ppermute | solution.py:18
  114.1 13.4 %collective-permute-start.6 = (bf16[16,8,1024]{2,1,0:T(8,128)(2,1)S(1)}, bf16[16,8,1024]{2,1,0:T(8,128)(2,1)S(1)}, u32[]{:S(2)}, u32[]{:S(2)}) collective-permute-start(bf16[16,8,1024]{2,1,0:T(8,128)(2,1)S(1)} %get-tuple-element.13), channel_id=1, source_target_pairs={{1,0},{2,1},{3,2},{4,3},{5,4},{6,5},{7,6},{8,7},{9,8},{10,9},{11,1... | collective-permute-start | bytes 786440 | tf_op jit(solution)/shard_map/ppermute | solution.py:18
  127.5 1.9 %collective-permute-start.7 = (bf16[16,8,1024]{2,1,0:T(8,128)(2,1)S(1)}, bf16[16,8,1024]{2,1,0:T(8,128)(2,1)S(1)}, u32[]{:S(2)}, u32[]{:S(2)}) collective-permute-start(bf16[16,8,1024]{2,1,0:T(8,128)(2,1)S(1)} %get-tuple-element.14), channel_id=1, source_target_pairs={{0,1},{1,2},{2,3},{3,4},{4,5},{5,6},{6,7},{7,8},{8,9},{9,10},{10,1... | collective-permute-start | bytes 786440 | tf_op jit(solution)/shard_map/ppermute | solution.py:18
  131.3 5.9 %collective-permute-done.7 = bf16[16,8,1024]{2,1,0:T(8,128)(2,1)S(1)} collective-permute-done((bf16[16,8,1024]{2,1,0:T(8,128)(2,1)S(1)}, bf16[16,8,1024]{2,1,0:T(8,128)(2,1)S(1)}, u32[]{:S(2)}, u32[]{:S(2)}) %collective-permute-start.7) | collective-permute-done | bytes 262176 | tf_op jit(solution)/shard_map/ppermute | solution.py:18
  147.5 2.8 %fusion.4 = bf16[16,8,1024]{2,1,0:T(8,128)(2,1)} fusion(bf16[1024,1536]{1,0:T(8,128)(2,1)S(1)} %copy-done, bf16[128,512]{1,0:T(8,128)(2,1)} %slice.134, bf16[128,512]{1,0:T(8,128)(2,1)S(1)} %multiply_convert_fusion.1, bf16[128,512]{1,0:T(8,128)(2,1)} %copy.37), kind=kOutput, calls=%fused_computation.14 | convolution fusion | flops 403963904 | bytes 3801088 | tf_op jit(solution)/shard_map/nf,df->nd/dot_general | solution.py:162
  (90 shorter events, 50.0 us)
Async XLA Ops:
  0.0 1.9 %copy-start = (bf16[1024,1536]{1,0:T(8,128)(2,1)S(1)}, bf16[1024,1536]{1,0:T(8,128)(2,1)}, u32[]{:S(2)}) copy-start(bf16[1024,1536]{1,0:T(8,128)(2,1)} %param.6) | copy-start | bytes 9437188
  0.0 5.1 %copy-start.14 = (f32[8]{0:T(128)S(1)}, f32[8]{0:T(128)}, u32[]{:S(2)}) copy-start(f32[8]{0:T(128)} %param.8) | copy-start | bytes 100
  3.4 1.0 copy-start.2
  5.1 0.6 copy-start.12
  17.3 18.7 %collective-permute-start = (bf16[8,8,1024]{2,1,0:T(8,128)(2,1)}, bf16[8,8,1024]{2,1,0:T(8,128)(2,1)}, u32[]{:S(2)}, u32[]{:S(2)}) collective-permute-start(bf16[8,8,1024]{2,1,0:T(8,128)(2,1)} %get-tuple-element.17), channel_id=1, source_target_pairs={{0,32},{32,64},{64,96},{96,128},{128,160},{160,192},{192,224},{224... | collective-permute-start | bytes 393224 | tf_op jit(solution)/shard_map/ppermute | solution.py:28
  22.0 17.0 %collective-permute-start.1 = (bf16[8,8,1024]{2,1,0:T(8,128)(2,1)}, bf16[8,8,1024]{2,1,0:T(8,128)(2,1)}, u32[]{:S(2)}, u32[]{:S(2)}) collective-permute-start(bf16[8,8,1024]{2,1,0:T(8,128)(2,1)} %get-tuple-element.18), channel_id=1, source_target_pairs={{32,0},{64,32},{96,64},{128,96},{160,128},{192,160},{224,192},{256... | collective-permute-start | bytes 393224 | tf_op jit(solution)/shard_map/ppermute | solution.py:29
  36.0 3.0 %copy-start.8 = (bf16[16,8,1024]{2,1,0:T(8,128)(2,1)}, bf16[16,8,1024]{2,1,0:T(8,128)(2,1)S(1)}, u32[]{:S(2)}) copy-start(bf16[16,8,1024]{2,1,0:T(8,128)(2,1)S(1)} %fusion.16) | copy-start | bytes 786436
  40.9 10.3 %collective-permute-start.3 = (bf16[32,8,1024]{2,1,0:T(8,128)(2,1)}, bf16[32,8,1024]{2,1,0:T(8,128)(2,1)}, u32[]{:S(2)}, u32[]{:S(2)}) collective-permute-start(bf16[32,8,1024]{2,1,0:T(8,128)(2,1)} %pad_maximum_fusion.2), channel_id=1, source_target_pairs={{1,0},{2,1},{3,2},{4,3},{5,4},{6,5},{7,6},{8,7},{9,8},{10,9},{11,1... | collective-permute-start | bytes 1572872 | tf_op jit(solution)/shard_map/ppermute | solution.py:29
  42.9 12.9 %collective-permute-start.2 = (bf16[32,8,1024]{2,1,0:T(8,128)(2,1)}, bf16[32,8,1024]{2,1,0:T(8,128)(2,1)}, u32[]{:S(2)}, u32[]{:S(2)}) collective-permute-start(bf16[32,8,1024]{2,1,0:T(8,128)(2,1)} %pad_maximum_fusion.2), channel_id=1, source_target_pairs={{0,1},{1,2},{2,3},{3,4},{4,5},{5,6},{6,7},{7,8},{8,9},{9,10},{10,1... | collective-permute-start | bytes 1572872 | tf_op jit(solution)/shard_map/ppermute | solution.py:28
  57.3 5.9 %copy-start.15 = (f32[8]{0:T(128)S(1)}, f32[8]{0:T(128)}, u32[]{:S(2)}) copy-start(f32[8]{0:T(128)} %param.8) | copy-start | bytes 100
  63.2 2.2 %copy-start.10 = (bf16[128,512]{0,1:T(8,128)(2,1)S(1)}, bf16[128,512]{0,1:T(8,128)(2,1)}, u32[]{:S(2)}) copy-start(bf16[128,512]{0,1:T(8,128)(2,1)} %copy.29) | copy-start | bytes 393220
  63.2 2.2 %copy-start.11 = (pred[128,768]{1,0:T(8,128)(4,1)S(1)}, pred[128,768]{1,0:T(8,128)(4,1)}, u32[]{:S(2)}) copy-start(pred[128,768]{1,0:T(8,128)(4,1)} %and.127) | copy-start | bytes 294916
  65.4 1.1 copy-start.9
  66.5 3.9 %copy-start.5 = (f32[8,64,768]{2,1,0:T(8,128)}, f32[8,64,768]{2,1,0:T(8,128)S(1)}, u32[]{:S(2)}) copy-start(f32[8,64,768]{2,1,0:T(8,128)S(1)} %fusion.6) | copy-start | bytes 4718596
  68.9 1.2 copy-start.3
  70.4 1.5 %copy-start.1 = (f32[8,64,768]{2,1,0:T(8,128)}, f32[8,64,768]{2,1,0:T(8,128)S(1)}, u32[]{:S(2)}) copy-start(f32[8,64,768]{2,1,0:T(8,128)S(1)} %fusion.33) | copy-start | bytes 4718596
  76.0 27.1 %collective-permute-start.5 = (bf16[8,24,1024]{2,1,0:T(8,128)(2,1)}, bf16[8,24,1024]{2,1,0:T(8,128)(2,1)}, u32[]{:S(2)}, u32[]{:S(2)}) collective-permute-start(bf16[8,24,1024]{2,1,0:T(8,128)(2,1)} %bitcast.80), channel_id=1, source_target_pairs={{0,32},{32,64},{64,96},{96,128},{128,160},{160,192},{192,224},{224... | collective-permute-start | bytes 1179656 | tf_op jit(solution)/shard_map/ppermute | solution.py:18
  81.3 30.8 %collective-permute-start.4 = (bf16[8,24,1024]{2,1,0:T(8,128)(2,1)}, bf16[8,24,1024]{2,1,0:T(8,128)(2,1)}, u32[]{:S(2)}, u32[]{:S(2)}) collective-permute-start(bf16[8,24,1024]{2,1,0:T(8,128)(2,1)} %bitcast.79), channel_id=1, source_target_pairs={{32,0},{64,32},{96,64},{128,96},{160,128},{192,160},{224,192},{256... | collective-permute-start | bytes 1179656 | tf_op jit(solution)/shard_map/ppermute | solution.py:18
  92.0 37.4 %copy-start.4 = (bf16[8,128,768]{2,1,0:T(8,128)(2,1)S(1)}, bf16[8,128,768]{2,1,0:T(8,128)(2,1)}, u32[]{:S(2)}) copy-start(bf16[8,128,768]{2,1,0:T(8,128)(2,1)} %copy-done.3) | copy-start | bytes 4718596
  92.0 37.4 %copy-start.6 = (bf16[768,512]{0,1:T(8,128)(2,1)S(1)}, bf16[768,512]{0,1:T(8,128)(2,1)}, u32[]{:S(2)}) copy-start(bf16[768,512]{0,1:T(8,128)(2,1)} %copy.38) | copy-start | bytes 2359300
  114.1 17.2 %collective-permute-start.6 = (bf16[16,8,1024]{2,1,0:T(8,128)(2,1)S(1)}, bf16[16,8,1024]{2,1,0:T(8,128)(2,1)S(1)}, u32[]{:S(2)}, u32[]{:S(2)}) collective-permute-start(bf16[16,8,1024]{2,1,0:T(8,128)(2,1)S(1)} %get-tuple-element.13), channel_id=1, source_target_pairs={{1,0},{2,1},{3,2},{4,3},{5,4},{6,5},{7,6},{8,7},{9,8},{10,9},{11,1... | collective-permute-start | bytes 786440 | tf_op jit(solution)/shard_map/ppermute | solution.py:18
  127.5 15.2 %copy-start.13 = (f32[8]{0:T(128)S(1)}, f32[8]{0:T(128)}, u32[]{:S(2)}) copy-start(f32[8]{0:T(128)} %copy-done.12) | copy-start | bytes 100
  127.5 9.8 %collective-permute-start.7 = (bf16[16,8,1024]{2,1,0:T(8,128)(2,1)S(1)}, bf16[16,8,1024]{2,1,0:T(8,128)(2,1)S(1)}, u32[]{:S(2)}, u32[]{:S(2)}) collective-permute-start(bf16[16,8,1024]{2,1,0:T(8,128)(2,1)S(1)} %get-tuple-element.14), channel_id=1, source_target_pairs={{0,1},{1,2},{2,3},{3,4},{4,5},{5,6},{6,7},{7,8},{8,9},{9,10},{10,1... | collective-permute-start | bytes 786440 | tf_op jit(solution)/shard_map/ppermute | solution.py:18
  137.4 0.9 copy-start.7
where the time goes:
time: 152 us; the launch traced here: 150 us
  starting transfers between devices  39.1 us (26%)
  local copies, waits for them, and re-layouts  36.8 us (24%)
  waiting for transfers between devices  34.3 us (23%)
  other arithmetic  25.8 us (17%)
  matrix products  13.9 us (9%)
    ppermute x4, waiting for transfers between devices, passed_along(): lax.ppermute(value, axis, [(source, source + steps) for source in range(i...  26.7 us
    ppermute x4, starting transfers between devices, passed_along(): lax.ppermute(value, axis, [(source, source + steps) for source in range(i...  25 us
    unnamed x34, local copies, waits for them, and re-layouts  8.69 us
    ppermute x2, starting transfers between devices, extended(): before = lax.ppermute(last, axis, up)  7.04 us
    ppermute x2, starting transfers between devices, extended(): after = lax.ppermute(initial, axis, down)  7.02 us
    mul x6, local copies, waits for them, and re-layouts, unit_heads(): scaled = shaped * jnp.sqrt(head_scale)[:, None] * lax.rsqrt(squares)  5.13 us
    ppermute x2, waiting for transfers between devices, extended(): before = lax.ppermute(last, axis, up)  4.64 us
    another operation x4, other arithmetic  4.29 us
  transfers between devices with their start and end apart: 8, of which 6 were waited for; matrix products, arithmetic and copies ran while one was open for 15% of the time, Pallas kernels for 0%

commit v1 on v0

v1 whole, which is shorter than its diff:
```python
import jax
import jax.numpy as jnp
from jax import lax
from jax.experimental import pallas as pl
from jax.experimental.pallas import tpu as pltpu
from jax.sharding import PartitionSpec as P

D = 1024
HEADS = 8
HEAD_DIM = 64
RADIUS = 8
PAIRS = HEADS // 2
PAIR = 2 * HEAD_DIM
WIDTH = HEADS * HEAD_DIM
TILE_H = 16
TILE_W = 8
OWN = TILE_H * TILE_W
HALF = OWN // 2
GROUP = 3 * OWN

norm_epsilon = 1e-06

MESH = pl.DeviceIdType.MESH
F32 = jnp.float32
BF16 = jnp.bfloat16
AROUND = [(dr, dc) for dr in (-1, 0, 1) for dc in (-1, 0, 1) if (dr, dc) != (0, 0)]


def slot_of(dr, dc):
    return (dr + 1) * 3 + (dc + 1)


def dot(a, b):
    return lax.dot_general(a, b, (((1,), (0,)), ((), ())), preferred_element_type=F32)


def dot_nt(a, b):
    return lax.dot_general(a, b, (((1,), (1,)), ((), ())), preferred_element_type=F32)


def head_sums(array, ones):
    high = array.astype(BF16)
    low = (array - high.astype(F32)).astype(BF16)
    return dot(high, ones) + dot(low, ones)


def kernel(
    scale_ref, x_hbm, w_hbm, ow_hbm, cot_hbm, out_ref,
    xa, xb, da, db, w, ow, cot,
    qa, ka, va, qb, kb, vb,
    qm, km, vm, dm, qraw, kraw,
    mask_a, mask_b,
    ea, pa, eb, pb, fa, ga, fb, gb,
    zbc, dbc, zmine, znear, za, zb,
    dqkv,
    local_sem, ys, yr, cs, cr, fs, fr, zs, zr,
):
    nrow, ncol = lax.axis_size("row"), lax.axis_size("col")
    r, c = lax.axis_index("row"), lax.axis_index("col")

    def has(dr, dc):
        ok = None
        for at, d, n in ((r, dr, nrow), (c, dc, ncol)):
            if d:
                here = at > 0 if d < 0 else at < n - 1
                ok = here if ok is None else jnp.logical_and(ok, here)
        return ok

    def device(dr, dc):
        return (jnp.clip(r + dr, 0, nrow - 1), jnp.clip(c + dc, 0, ncol - 1))

    def remote(src, dst, send, recv, dr, dc):
        return pltpu.make_async_remote_copy(
            src_ref=src, dst_ref=dst, send_sem=send, recv_sem=recv,
            device_id=device(dr, dc), device_id_type=MESH,
        )

    barrier = pltpu.get_barrier_semaphore()
    count = 0
    for dr, dc in AROUND:
        there = has(dr, dc)
        count = count + there.astype(jnp.int32)

        @pl.when(there)
        def _():
            pl.semaphore_signal(barrier, inc=1, device_id=device(dr, dc), device_id_type=MESH)

    local = [
        pltpu.make_async_copy(src, dst, local_sem.at[i])
        for i, (src, dst) in enumerate(((cot_hbm, cot), (ow_hbm, ow), (x_hbm, xa.at[1]), (w_hbm, w)))
    ]
    for copy in local:
        copy.start()

    def top(n):
        return pl.ds(0, HALF) if n == 0 else pl.ds(HALF, HALF)

    def y_copy(kind, dr):
        src, dst = (x_hbm, xb) if kind == 0 else (da.at[1], db)
        mine, theirs = (0, 1) if dr < 0 else (1, 0)
        i = 2 * kind + (dr > 0)
        return remote(src.at[top(mine)], dst.at[1, top(theirs)], ys.at[i], yr.at[i], dr, 0)

    def c_copy(kind, dc):
        src, dst = (x_hbm, xa) if kind == 0 else (da.at[1], da)
        i = 2 * kind + (dc > 0)
        return remote(src, dst.at[0 if dc > 0 else 2], cs.at[i], cr.at[i], 0, dc)

    def f_copy(kind, half, dc):
        buf = xb if kind == 0 else db
        i = 4 * kind + 2 * half + (dc > 0)
        return remote(
            buf.at[1, top(half)], buf.at[0 if dc > 0 else 2, top(half)], fs.at[i], fr.at[i], 0, dc
        )

    def z_copy(dr, dc):
        i = slot_of(dr, dc)
        return remote(zmine, znear.at[slot_of(-dr, -dc)], zs.at[i], zr.at[i], dr, dc)

    def halo_from(half):
        return has(-1, 0) if half == 0 else has(1, 0)

    pl.semaphore_wait(barrier, count)
    for dr in (-1, 1):

        @pl.when(has(dr, 0))
        def _():
            y_copy(0, dr).start()

    for dc in (-1, 1):

        @pl.when(has(0, dc))
        def _():
            c_copy(0, dc).start()

    for dc in (-1, 1):

        @pl.when(jnp.logical_not(has(0, dc)))
        def _():
            b = 1 + dc
            xa[b] = jnp.zeros((OWN, D), BF16)
            da[b] = jnp.zeros((OWN, WIDTH), BF16)
            xb[b] = jnp.zeros((OWN, D), BF16)
            db[b] = jnp.zeros((OWN, WIDTH), BF16)

    for half in (0, 1):

        @pl.when(jnp.logical_not(halo_from(half)))
        def _():
            for b in range(3):
                xb[b, top(half)] = jnp.zeros((HALF, D), BF16)
                db[b, top(half)] = jnp.zeros((HALF, WIDTH), BF16)

    for dr, dc in AROUND:

        @pl.when(jnp.logical_not(has(dr, dc)))
        def _():
            znear[slot_of(dr, dc)] = jnp.zeros((2 * HEADS, OWN), F32)

    local[0].wait()
    local[1].wait()
    for n in range(2):
        cols = pl.ds(256 * n, 256)
        da[1, :, cols] = dot(cot[...], ow[:, cols]).astype(BF16)
    for dr in (-1, 1):

        @pl.when(has(dr, 0))
        def _():
            y_copy(1, dr).start()

    for dc in (-1, 1):

        @pl.when(has(0, dc))
        def _():
            c_copy(1, dc).start()

    def head_ones(n):
        a = lax.broadcasted_iota(jnp.int32, (n, n), 0) // HEAD_DIM
        b = lax.broadcasted_iota(jnp.int32, (n, n), 1) // HEAD_DIM
        return jnp.where(a == b, 1.0, 0.0).astype(BF16)

    def scale_row(first, heads):
        lane = lax.broadcasted_iota(jnp.int32, (1, heads * HEAD_DIM), 1) // HEAD_DIM
        row = jnp.zeros((1, heads * HEAD_DIM), F32)
        for h in range(heads):
            row = jnp.where(lane == h, scale_ref[first + h], row)
        return jnp.sqrt(row)

    quad_rows = [scale_row(0, 4), scale_row(4, 4)]
    own = lax.broadcasted_iota(jnp.int32, (OWN, GROUP), 0)
    other = lax.broadcasted_iota(jnp.int32, (OWN, GROUP), 1)
    own_i, own_j = own // TILE_W, own % TILE_W
    there_i = (other % OWN) // TILE_W
    there_j = other % TILE_W + TILE_W * (other // OWN - 1)
    col_at = c * TILE_W + there_j
    cols_ok = (jnp.abs(there_j - own_j) <= RADIUS) & (col_at >= 0) & (col_at < ncol * TILE_W)
    mask_a[...] = jnp.where((jnp.abs(there_i - own_i) <= RADIUS) & cols_ok, 1.0, 0.0)
    halo_i = jnp.where(there_i < RADIUS, there_i - RADIUS, there_i - RADIUS + TILE_H)
    row_at = r * TILE_H + halo_i
    rows_ok = (jnp.abs(halo_i - own_i) <= RADIUS) & (row_at >= 0) & (row_at < nrow * TILE_H)
    mask_b[...] = jnp.where(rows_ok & cols_ok, 1.0, 0.0)

    def project(x_block, q_to, k_to, v_to, rows, raw=False):
        ones = head_ones(256)
        for n in range(6):
            cols = pl.ds(256 * n, 256)
            values = dot(x_block[...], w[:, cols])
            kind, quad = n // 2, n % 2
            if kind < 2:
                if raw:
                    keep = qraw if kind == 0 else kraw
                    keep[:, pl.ds(256 * quad, 256)] = values
                squares = head_sums(values * values, ones) + norm_epsilon
                values = values * quad_rows[quad] * lax.rsqrt(squares)
            result = values.astype(BF16)
            to = (q_to, k_to, v_to)[kind]
            to[2 * quad, rows] = result[:, :PAIR]
            to[2 * quad + 1, rows] = result[:, PAIR:]

    local[2].wait()
    local[3].wait()
    project(xa.at[1], qa, ka, va, pl.ds(OWN, OWN), raw=True)
    first_half = lax.broadcasted_iota(jnp.int32, (OWN, PAIR), 1) < HEAD_DIM
    zero = jnp.zeros((OWN, PAIR), BF16)
    for p in range(PAIRS):
        mine = pl.ds(OWN, OWN)
        for to, values in (
            (qm, qa[p, mine]), (km, ka[p, mine]), (vm, va[p, mine]), (dm, da[1, :, pl.ds(PAIR * p, PAIR)]),
        ):
            to[2 * p] = jnp.where(first_half, values, zero)
            to[2 * p + 1] = jnp.where(first_half, zero, values)

    for dc in (-1, 1):

        @pl.when(has(0, -dc))
        def _():
            c_copy(0, dc).wait_recv()

    def project_sides(x_buf, q_to, k_to, v_to):
        def body(i, carry):
            b = 2 * i
            rows = pl.ds(pl.multiple_of(b * OWN, OWN), OWN)
            project(x_buf.at[b], q_to, k_to, v_to, rows)
            return carry

        lax.fori_loop(0, 2, body, 0)

    project_sides(xa, qa, ka, va)

    def query_first(k_of, v_of, mask, e_to, p_to):
        def body(h, carry):
            p = h // 2
            e = jnp.exp(dot_nt(qm[h], k_of[p])) * mask[...]
            e_to[h] = e
            p_to[h] = dot_nt(dm[h], v_of[p])
            return carry

        lax.fori_loop(0, HEADS, body, 0)

    query_first(ka, va, mask_a, ea, pa)

    for dc in (-1, 1):

        @pl.when(has(0, -dc))
        def _():
            c_copy(1, dc).wait_recv()

    def key_first(q_of, d_of, mask, e_to, p_to):
        def body(h, carry):
            p = h // 2
            e_to[h] = jnp.exp(dot_nt(km[h], q_of[p])) * mask[...]
            cols = pl.ds(pl.multiple_of(p * PAIR, PAIR), PAIR)
            for b in range(3):
                p_to[h, :, pl.ds(b * OWN, OWN)] = dot_nt(vm[h], d_of[b, :, cols])
            return carry

        lax.fori_loop(0, HEADS, body, 0)

    key_first(qa, da, mask_a, fa, ga)

    def pass_on(kind):
        for half, dr in ((0, 1), (1, -1)):

            @pl.when(halo_from(half))
            def _():
                y_copy(kind, dr).wait_recv()
                for dc in (-1, 1):

                    @pl.when(has(0, dc))
                    def _():
                        f_copy(kind, half, dc).start()

    def corners(kind):
        for half in (0, 1):
            for dc in (-1, 1):

                @pl.when(jnp.logical_and(halo_from(half), has(0, -dc)))
                def _():
                    f_copy(kind, half, dc).wait_recv()

    pass_on(0)
    project(xb.at[1], qb, kb, vb, pl.ds(OWN, OWN))
    corners(0)
    project_sides(xb, qb, kb, vb)
    query_first(kb, vb, mask_b, eb, pb)

    lane = lax.broadcasted_iota(jnp.int32, (OWN, OWN), 1)

    def totals(h, table):
        z = jnp.sum(ea[h] + eb[h], axis=1, keepdims=True)
        along = jnp.sum(ea[h] * pa[h] + eb[h] * pb[h], axis=1, keepdims=True)
        inverse = 1.0 / z
        delta = along * inverse
        zbc[h] = jnp.broadcast_to(inverse, (OWN, OWN))
        dbc[h] = jnp.broadcast_to(delta, (OWN, OWN))
        table = jnp.where(lane == h, inverse, table)
        return jnp.where(lane == HEADS + h, delta, table)

    table = lax.fori_loop(0, HEADS, totals, jnp.zeros((OWN, OWN), F32))
    zmine[...] = table.T[: 2 * HEADS]
    for dr, dc in AROUND:

        @pl.when(has(dr, dc))
        def _():
            z_copy(dr, dc).start()

    pass_on(1)

    def per_pair(one_head):
        def body(p, carry):
            parts = [one_head(2 * p), one_head(2 * p + 1)]
            for n in range(len(parts[0])):
                kind, _ = parts[0][n]
                dqkv[kind, p] = jnp.where(first_half, parts[0][n][1], parts[1][n][1])
            return carry

        lax.fori_loop(0, PAIRS, body, 0)

    def query_second(h):
        p = h // 2
        result = jnp.zeros((OWN, PAIR), F32)
        inverse = jnp.concatenate([zbc[h]] * 3, axis=1)
        delta = jnp.concatenate([dbc[h]] * 3, axis=1)
        for e, dp, keys in ((ea, pa, ka), (eb, pb, kb)):
            dscore = (e[h] * inverse * (dp[h] - delta)).astype(BF16)
            result = result + dot(dscore, keys[p])
        return [(0, result)]

    per_pair(query_second)

    corners(1)
    key_first(qb, db, mask_b, fb, gb)
    for dr, dc in AROUND:

        @pl.when(has(dr, dc))
        def _():
            z_copy(-dr, -dc).wait_recv()

    znear[slot_of(0, 0)] = zmine[...]
    below = lax.broadcasted_iota(jnp.int32, (2 * HEADS, OWN), 1) < HALF
    for b in range(3):
        cols = pl.ds(b * OWN, OWN)
        za[:, cols] = znear[slot_of(0, b - 1)]
        up, down = znear[slot_of(-1, b - 1)], znear[slot_of(1, b - 1)]
        zb[:, cols] = pltpu.roll(jnp.where(below, down, up), HALF, 1)

    def key_second(h):
        p = h // 2
        dkey = jnp.zeros((OWN, PAIR), F32)
        dvalue = jnp.zeros((OWN, PAIR), F32)
        cols = pl.ds(pl.multiple_of(p * PAIR, PAIR), PAIR)
        for e, dp, queries, cots, table in ((fa, ga, qa, da, za), (fb, gb, qb, db, zb)):
            probs = e[h] * table[pl.ds(h, 1), :]
            dscore = (probs * (dp[h] - table[pl.ds(HEADS + h, 1), :])).astype(BF16)
            dkey = dkey + dot(dscore, queries[p])
            probs_bf = probs.astype(BF16)
            for b in range(3):
                dvalue = dvalue + dot(probs_bf[:, b * OWN : (b + 1) * OWN], cots[b, :, cols])
        return [(1, dkey), (2, dvalue)]

    per_pair(key_second)

    ones = head_ones(PAIR)
    total = jnp.zeros((OWN, D), F32)
    for kind in range(3):
        for p in range(PAIRS):
            grads = dqkv[kind, p]
            cols = pl.ds(PAIR * p, PAIR)
            if kind < 2:
                raw = (qraw if kind == 0 else kraw)[:, cols]
                squares = head_sums(raw * raw, ones) + norm_epsilon
                along = head_sums(grads * raw, ones) / squares
                row = quad_rows[p // 2][:, PAIR * (p % 2) : PAIR * (p % 2 + 1)]
                grads = row * lax.rsqrt(squares) * (grads - raw * along)
            qm[p] = grads.astype(BF16)
        block = jnp.concatenate([qm[p] for p in range(PAIRS)], axis=1)
        total = total + dot_nt(block, w[:, pl.ds(WIDTH * kind, WIDTH)])
    out_ref[...] = total.astype(BF16)

    for kind in (0, 1):
        for dr in (-1, 1):

            @pl.when(has(dr, 0))
            def _():
                y_copy(kind, dr).wait_send()

        for dc in (-1, 1):

            @pl.when(has(0, dc))
            def _():
                c_copy(kind, dc).wait_send()

            for half in (0, 1):

                @pl.when(jnp.logical_and(halo_from(half), has(0, dc)))
                def _():
                    f_copy(kind, half, dc).wait_send()

    for dr, dc in AROUND:

        @pl.when(has(dr, dc))
        def _():
            z_copy(dr, dc).wait_send()


def per_device(grid_input, w_qkv, out_weight, head_scale, cotangent):
    dma = pltpu.SemaphoreType.DMA
    heads_mine = pltpu.VMEM((HEADS, OWN, PAIR), BF16)
    by_pair = pltpu.VMEM((PAIRS, GROUP, PAIR), BF16)
    scores = pltpu.VMEM((HEADS, OWN, GROUP), F32)
    any_space = pl.BlockSpec(memory_space=pl.ANY)
    result = pl.pallas_call(
        kernel,
        out_shape=jax.ShapeDtypeStruct((OWN, D), BF16),
        in_specs=[pl.BlockSpec(memory_space=pltpu.SMEM)] + [any_space] * 4,
        out_specs=pl.BlockSpec(memory_space=pltpu.VMEM),
        scratch_shapes=[
            pltpu.VMEM((3, OWN, D), BF16),
            pltpu.VMEM((3, OWN, D), BF16),
            pltpu.VMEM((3, OWN, WIDTH), BF16),
            pltpu.VMEM((3, OWN, WIDTH), BF16),
            pltpu.VMEM((D, 3 * WIDTH), BF16),
            pltpu.VMEM((D, WIDTH), BF16),
            pltpu.VMEM((OWN, D), BF16),
            *[by_pair] * 6,
            *[heads_mine] * 4,
            pltpu.VMEM((OWN, WIDTH), F32),
            pltpu.VMEM((OWN, WIDTH), F32),
            pltpu.VMEM((OWN, GROUP), F32),
            pltpu.VMEM((OWN, GROUP), F32),
            *[scores] * 8,
            pltpu.VMEM((HEADS, OWN, OWN), F32),
            pltpu.VMEM((HEADS, OWN, OWN), F32),
            pltpu.VMEM((2 * HEADS, OWN), F32),
            pltpu.VMEM((9, 2 * HEADS, OWN), F32),
            pltpu.VMEM((2 * HEADS, GROUP), F32),
            pltpu.VMEM((2 * HEADS, GROUP), F32),
            pltpu.VMEM((3, PAIRS, OWN, PAIR), F32),
            dma((4,)),
            dma((4,)),
            dma((4,)),
            dma((4,)),
            dma((4,)),
            dma((8,)),
            dma((8,)),
            dma((9,)),
            dma((9,)),
        ],
        compiler_params=pltpu.CompilerParams(
            collective_id=0, has_side_effects=True, vmem_limit_bytes=48 << 20
        ),
    )(
        head_scale,
        grid_input.reshape(OWN, D),
        w_qkv,
        out_weight,
        cotangent.reshape(OWN, D),
    )
    return result.reshape(TILE_H, TILE_W, D)


def solution(mesh):
    placed = (P("row", "col", None), P(), P(), P(), P("row", "col", None))
    return jax.shard_map(
        per_device, mesh=mesh, in_specs=placed, out_specs=P("row", "col", None), check_vma=False
    )
```

time: 152 us -> 63.9 us (0.42)
  the two profiles are of different devices: /device:TPU:168 before, /device:TPU:455 now
where the time goes in v1:
time: 63.9 us; the launch traced here: 63.7 us
  Pallas kernels  57.3 us (90%)
  local copies, waits for them, and re-layouts  6.37 us (10%)
    pallas_call x1, Pallas kernels, per_device(): pl.pallas_call(kernel, out_shape=jax.ShapeDtypeStruct((OWN, D), BF16), in...  57.3 us
    unnamed x11, local copies, waits for them, and re-layouts  6.37 us

profile of v1, /device:TPU:455, one launch (start us, length us, event | category | flops | bytes accessed | tf_op | source)
XLA Modules:
  0.0 63.7 jit_solution(11401816944247384200)
XLA Ops:
  0.0 0.0 copy-start
  0.0 1.9 %copy-done = bf16[1024,1536]{1,0:T(8,128)(2,1)S(1)} copy-done((bf16[1024,1536]{1,0:T(8,128)(2,1)S(1)}, bf16[1024,1536]{1,0:T(8,128)(2,1)}, u32[]{:S(2)}) %copy-start) | copy-done | bytes 3145752
  1.9 0.0 copy-start.1
  1.9 1.2 %copy-done.1 = bf16[1024,512]{1,0:T(8,128)(2,1)S(1)} copy-done((bf16[1024,512]{1,0:T(8,128)(2,1)S(1)}, bf16[1024,512]{1,0:T(8,128)(2,1)}, u32[]{:S(2)}) %copy-start.1) | copy-done | bytes 1048600
  3.1 0.0 copy-start.2
  3.1 0.9 %copy-done.2 = bf16[16,8,1024]{2,1,0:T(8,128)(2,1)S(1)} copy-done((bf16[16,8,1024]{2,1,0:T(8,128)(2,1)S(1)}, bf16[16,8,1024]{2,1,0:T(8,128)(2,1)}, u32[]{:S(2)}) %copy-start.2) | copy-done | bytes 262168
  4.1 0.0 copy-start.3
  4.1 0.9 %copy-done.3 = bf16[16,8,1024]{2,1,0:T(8,128)(2,1)S(1)} copy-done((bf16[16,8,1024]{2,1,0:T(8,128)(2,1)S(1)}, bf16[16,8,1024]{2,1,0:T(8,128)(2,1)}, u32[]{:S(2)}) %copy-start.3) | copy-done | bytes 262168
  5.0 0.0 copy-start.4
  5.0 0.7 %copy-done.4 = f32[8]{0:T(128)S(1)} copy-done((f32[8]{0:T(128)S(1)}, f32[8]{0:T(128)}, u32[]{:S(2)}) %copy-start.4) | copy-done | bytes 56
  5.7 57.3 %shard_map.55 = bf16[128,1024]{1,0:T(8,128)(2,1)S(1)} custom-call(f32[8]{0:T(128)S(1)} %copy-done.4, bf16[128,1024]{1,0:T(8,128)(2,1)S(1)} %bitcast.4, bf16[1024,1536]{1,0:T(8,128)(2,1)S(1)} %copy-done, bf16[1024,512]{1,0:T(8,128)(2,1)S(1)} %copy-done.1, bf16[128,1024]{1,0:T(8,128)(2,1)S(1)} %bitcast.5), custom_call_target="tpu_custom_call" | custom-call | tf_op jit(solution)/shard_map/pallas_call | solution.py:432
  62.9 0.7 %copy.7 = bf16[16,8,1024]{2,1,0:T(8,128)(2,1)} copy(bf16[16,8,1024]{2,1,0:T(8,128)(2,1)S(1)} %bitcast.3) | data formatting | bytes 524288
Async XLA Ops:
  0.0 1.9 %copy-start = (bf16[1024,1536]{1,0:T(8,128)(2,1)S(1)}, bf16[1024,1536]{1,0:T(8,128)(2,1)}, u32[]{:S(2)}) copy-start(bf16[1024,1536]{1,0:T(8,128)(2,1)} %w_hbm.1) | copy-start | bytes 9437188
  1.9 1.2 %copy-start.1 = (bf16[1024,512]{1,0:T(8,128)(2,1)S(1)}, bf16[1024,512]{1,0:T(8,128)(2,1)}, u32[]{:S(2)}) copy-start(bf16[1024,512]{1,0:T(8,128)(2,1)} %ow_hbm.1) | copy-start | bytes 3145732
  3.1 0.9 %copy-start.2 = (bf16[16,8,1024]{2,1,0:T(8,128)(2,1)S(1)}, bf16[16,8,1024]{2,1,0:T(8,128)(2,1)}, u32[]{:S(2)}) copy-start(bf16[16,8,1024]{2,1,0:T(8,128)(2,1)} %param.5) | copy-start | bytes 786436
  4.1 0.9 %copy-start.3 = (bf16[16,8,1024]{2,1,0:T(8,128)(2,1)S(1)}, bf16[16,8,1024]{2,1,0:T(8,128)(2,1)}, u32[]{:S(2)}) copy-start(bf16[16,8,1024]{2,1,0:T(8,128)(2,1)} %param.9) | copy-start | bytes 786436
  5.0 0.7 %copy-start.4 = (f32[8]{0:T(128)S(1)}, f32[8]{0:T(128)}, u32[]{:S(2)}) copy-start(f32[8]{0:T(128)} %scale_ref.1) | copy-start | bytes 100

commit v2 on v1

v2 whole, which is shorter than its diff:
```python
import jax
import jax.numpy as jnp
from jax import lax
from jax.experimental import pallas as pl
from jax.experimental.pallas import tpu as pltpu
from jax.sharding import PartitionSpec as P

D = 1024
HEADS = 8
HEAD_DIM = 64
RADIUS = 8
PAIRS = HEADS // 2
PAIR = 2 * HEAD_DIM
WIDTH = HEADS * HEAD_DIM
TILE_H = 16
TILE_W = 8
OWN = TILE_H * TILE_W
HALF = OWN // 2
GROUP = 3 * OWN

norm_epsilon = 1e-06

MESH = pl.DeviceIdType.MESH
F32 = jnp.float32
BF16 = jnp.bfloat16
AROUND = [(dr, dc) for dr in (-1, 0, 1) for dc in (-1, 0, 1) if (dr, dc) != (0, 0)]


def slot_of(dr, dc):
    return (dr + 1) * 3 + (dc + 1)


def dot(a, b):
    return lax.dot_general(a, b, (((1,), (0,)), ((), ())), preferred_element_type=F32)


def dot_nt(a, b):
    return lax.dot_general(a, b, (((1,), (1,)), ((), ())), preferred_element_type=F32)


def head_sums(array, ones):
    high = array.astype(BF16)
    low = (array - high.astype(F32)).astype(BF16)
    return dot(high, ones) + dot(low, ones)


def kernel(
    scale_hbm, x_hbm, w_hbm, ow_hbm, cot_hbm, out_ref,
    scale_ref, xa, xb, da, db, w, ow, cot,
    qa, ka, va, qb, kb, vb,
    qm, km, vm, dm, raws, back_own, back_raw,
    mask_a, mask_b,
    ea, pa, eb, pb, fa, ga, fb, gb,
    zpart, apart, zbc, dbc, zmine, znear, za, zb,
    dqkv, partial,
    local_sem, ys, yr, cs, cr, fs, fr, zs, zr,
):
    nrow, ncol = lax.axis_size("row"), lax.axis_size("col")
    r, c = lax.axis_index("row"), lax.axis_index("col")

    def has(dr, dc):
        ok = None
        for at, d, n in ((r, dr, nrow), (c, dc, ncol)):
            if d:
                here = at > 0 if d < 0 else at < n - 1
                ok = here if ok is None else jnp.logical_and(ok, here)
        return ok

    def device(dr, dc):
        return (jnp.clip(r + dr, 0, nrow - 1), jnp.clip(c + dc, 0, ncol - 1))

    def remote(src, dst, send, recv, dr, dc):
        return pltpu.make_async_remote_copy(
            src_ref=src, dst_ref=dst, send_sem=send, recv_sem=recv,
            device_id=device(dr, dc), device_id_type=MESH,
        )

    barrier = pltpu.get_barrier_semaphore()
    count = 0
    for dr, dc in AROUND:
        there = has(dr, dc)
        count = count + there.astype(jnp.int32)

        @pl.when(there)
        def _():
            pl.semaphore_signal(barrier, inc=1, device_id=device(dr, dc), device_id_type=MESH)

    local = [
        pltpu.make_async_copy(src, dst, local_sem.at[i])
        for i, (src, dst) in enumerate(
            ((cot_hbm, cot), (ow_hbm, ow), (x_hbm, xa.at[0]), (w_hbm, w), (scale_hbm, scale_ref))
        )
    ]
    for copy in local:
        copy.start()

    def block_of(dc):
        return 0 if dc == 0 else (1 if dc < 0 else 2)

    def half(n):
        return pl.ds(HALF * n, HALF)

    def y_copy(kind, dr):
        mine = 0 if dr < 0 else 1
        src, dst = (x_hbm, xb.at[0, half(1 - mine)]) if kind == 0 else (da.at[0], db.at[1 - mine, half(0)])
        i = 2 * kind + (dr > 0)
        return remote(src.at[half(mine)], dst, ys.at[i], yr.at[i], dr, 0)

    def c_copy(kind, dc):
        src, dst = (x_hbm, xa) if kind == 0 else (da.at[0], da)
        i = 2 * kind + (dc > 0)
        return remote(src, dst.at[block_of(-dc)], cs.at[i], cr.at[i], 0, dc)

    def f_copy(kind, n, dc):
        i = 4 * kind + 2 * n + (dc > 0)
        b = block_of(-dc)
        if kind == 0:
            src, dst = xb.at[0, half(n)], xb.at[b, half(n)]
        else:
            src, dst = db.at[n, half(0)], db.at[n, half(b)]
        return remote(src, dst, fs.at[i], fr.at[i], 0, dc)

    def z_copy(dr, dc):
        i = slot_of(dr, dc)
        return remote(zmine, znear.at[slot_of(-dr, -dc)], zs.at[i], zr.at[i], dr, dc)

    def halo_from(n):
        return has(-1, 0) if n == 0 else has(1, 0)

    pl.semaphore_wait(barrier, count)
    for dr in (-1, 1):

        @pl.when(has(dr, 0))
        def _():
            y_copy(0, dr).start()

    for dc in (-1, 1):

        @pl.when(has(0, dc))
        def _():
            c_copy(0, dc).start()

    for dc in (-1, 1):

        @pl.when(jnp.logical_not(has(0, dc)))
        def _():
            b = block_of(dc)
            xa[b] = jnp.zeros((OWN, D), BF16)
            da[b] = jnp.zeros((OWN, WIDTH), BF16)
            xb[b] = jnp.zeros((OWN, D), BF16)
            for n in (0, 1):
                db[n, half(b)] = jnp.zeros((HALF, WIDTH), BF16)

    for n in (0, 1):

        @pl.when(jnp.logical_not(halo_from(n)))
        def _():
            for b in range(3):
                xb[b, half(n)] = jnp.zeros((HALF, D), BF16)
            db[n] = jnp.zeros((3 * HALF, WIDTH), BF16)

    for dr, dc in AROUND:

        @pl.when(jnp.logical_not(has(dr, dc)))
        def _():
            znear[slot_of(dr, dc)] = jnp.zeros((2 * HEADS, OWN), F32)

    local[0].wait()
    local[1].wait()
    for n in range(2):
        cols = pl.ds(256 * n, 256)
        da[0, :, cols] = dot(cot[...], ow[:, cols]).astype(BF16)
    for dr in (-1, 1):

        @pl.when(has(dr, 0))
        def _():
            y_copy(1, dr).start()

    for dc in (-1, 1):

        @pl.when(has(0, dc))
        def _():
            c_copy(1, dc).start()

    local[4].wait()
    local[2].wait()
    local[3].wait()

    def head_ones(n):
        a = lax.broadcasted_iota(jnp.int32, (n, n), 0) // HEAD_DIM
        b = lax.broadcasted_iota(jnp.int32, (n, n), 1) // HEAD_DIM
        return jnp.where(a == b, 1.0, 0.0).astype(BF16)

    def scale_row(first, heads):
        lane = lax.broadcasted_iota(jnp.int32, (1, heads * HEAD_DIM), 1) // HEAD_DIM
        row = jnp.zeros((1, heads * HEAD_DIM), F32)
        for h in range(heads):
            row = jnp.where(lane == h, scale_ref[first + h], row)
        return jnp.sqrt(row)

    quad_rows = [scale_row(0, 4), scale_row(4, 4)]
    ones256 = head_ones(256)

    def window(rows, first_half, lanes, block, halo):
        row = lax.broadcasted_iota(jnp.int32, (rows, lanes), 0)
        lane = lax.broadcasted_iota(jnp.int32, (rows, lanes), 1)
        own_i = (row // OWN + first_half) * RADIUS + (row % HALF) // TILE_W
        own_j = row % TILE_W
        b = lane // block
        there_i = (lane % block) // TILE_W
        if halo:
            there_i = there_i - RADIUS if first_half == 0 else there_i + TILE_H
        there_j = lane % TILE_W + jnp.where(b == 0, 0, jnp.where(b == 1, -TILE_W, TILE_W))
        row_at, col_at = r * TILE_H + there_i, c * TILE_W + there_j
        near = (jnp.abs(there_i - own_i) <= RADIUS) & (jnp.abs(there_j - own_j) <= RADIUS)
        inside = (row_at >= 0) & (row_at < nrow * TILE_H) & (col_at >= 0) & (col_at < ncol * TILE_W)
        return jnp.where(near & inside, 1.0, 0.0)

    mask_a[...] = window(2 * OWN, 0, GROUP, OWN, False)
    for n in (0, 1):
        mask_b[n] = window(OWN, n, 3 * HALF, HALF, True)

    def project(x_rows, store, own=False):
        for n in range(6):
            values = dot(x_rows, w[:, pl.ds(256 * n, 256)])
            kind, quad = n // 2, n % 2
            if kind < 2:
                if own:
                    squares = head_sums(values * values, ones256) + norm_epsilon
                    factor = quad_rows[quad] * lax.rsqrt(squares)
                    cols = pl.ds(256 * quad, 256)
                    raws[kind, :, cols] = values
                    back_own[kind, :, cols] = factor
                    back_raw[kind, :, cols] = factor * values / squares
                else:
                    squares = dot((values * values).astype(BF16), ones256) + norm_epsilon
                    factor = quad_rows[quad] * lax.rsqrt(squares)
                values = values * factor
            result = values.astype(BF16)
            store(kind, 2 * quad, result[:, :PAIR])
            store(kind, 2 * quad + 1, result[:, PAIR:])

    def store_a(first):
        def store(kind, p, result):
            (qa, ka, va)[kind][p, pl.ds(first, result.shape[0])] = result

        return store

    def store_b(first):
        def store(kind, p, result):
            to = (qb, kb, vb)[kind]
            for i in range(result.shape[0] // HALF):
                to[i % 2, p, half(first + i // 2)] = result[HALF * i : HALF * (i + 1)]

        return store

    project(xa[0], store_a(0), own=True)
    first_lanes = lax.broadcasted_iota(jnp.int32, (HALF, PAIR), 1) < HEAD_DIM
    zero = jnp.zeros((HALF, PAIR), BF16)
    for p in range(PAIRS):
        for to, values in (
            (qm, qa[p, pl.ds(0, OWN)]), (km, ka[p, pl.ds(0, OWN)]), (vm, va[p, pl.ds(0, OWN)]),
            (dm, da[0, :, pl.ds(PAIR * p, PAIR)]),
        ):
            for n in (0, 1):
                rows = values[HALF * n : HALF * (n + 1)]
                to[p, half(2 * n)] = jnp.where(first_lanes, rows, zero)
                to[p, half(2 * n + 1)] = jnp.where(first_lanes, zero, rows)

    for dc in (-1, 1):

        @pl.when(has(0, -dc))
        def _():
            c_copy(0, dc).wait_recv()

    project(xa[1:3].reshape(2 * OWN, D), store_a(OWN))

    def tiles(array):
        return array[:, :OWN] + array[:, OWN : 2 * OWN] + array[:, 2 * OWN :]

    def query_a(p, carry):
        e = jnp.exp(dot_nt(qm[p], ka[p])) * mask_a[...]
        dp = dot_nt(dm[p], va[p])
        ea[p] = e
        pa[p] = dp
        zpart[p] = tiles(e)
        apart[p] = tiles(e * dp)
        return carry

    lax.fori_loop(0, PAIRS, query_a, 0)

    def pass_on(kind):
        for n, dr in ((0, 1), (1, -1)):

            @pl.when(halo_from(n))
            def _():
                y_copy(kind, dr).wait_recv()
                for dc in (-1, 1):

                    @pl.when(has(0, dc))
                    def _():
                        f_copy(kind, n, dc).start()

    def corners(kind):
        for n in (0, 1):
            for dc in (-1, 1):

                @pl.when(jnp.logical_and(halo_from(n), has(0, -dc)))
                def _():
                    f_copy(kind, n, dc).wait_recv()

    pass_on(0)
    project(xb[0], store_b(0))

    for dc in (-1, 1):

        @pl.when(has(0, -dc))
        def _():
            c_copy(1, dc).wait_recv()

    def lanes_of(p):
        return pl.ds(pl.multiple_of(p * PAIR, PAIR), PAIR)

    def key_a(p, carry):
        fa[p] = jnp.exp(dot_nt(km[p], qa[p])) * mask_a[...]
        ga[p] = dot_nt(vm[p], da[:, :, lanes_of(p)].reshape(GROUP, PAIR))
        return carry

    lax.fori_loop(0, PAIRS, key_a, 0)

    corners(0)
    project(xb[1:3].reshape(2 * OWN, D), store_b(1))
    pass_on(1)

    lane = lax.broadcasted_iota(jnp.int32, (2 * OWN, OWN), 1)

    def query_b(p, table):
        z, along = [], []
        for n in (0, 1):
            rows = pl.ds(OWN * n, OWN)
            e = jnp.exp(dot_nt(qm[p, rows], kb[n, p])) * mask_b[n]
            dp = dot_nt(dm[p, rows], vb[n, p])
            eb[p, n] = e
            pb[p, n] = dp
            z.append(jnp.sum(e, axis=1, keepdims=True))
            along.append(jnp.sum(e * dp, axis=1, keepdims=True))
        z = jnp.concatenate(z, axis=0) + jnp.sum(zpart[p], axis=1, keepdims=True)
        along = jnp.concatenate(along, axis=0) + jnp.sum(apart[p], axis=1, keepdims=True)
        inverse = 1.0 / z
        delta = along * inverse
        zbc[p] = jnp.broadcast_to(inverse, (2 * OWN, OWN))
        dbc[p] = jnp.broadcast_to(delta, (2 * OWN, OWN))
        table = jnp.where(lane == p, inverse, table)
        return jnp.where(lane == PAIRS + p, delta, table)

    table = lax.fori_loop(0, PAIRS, query_b, jnp.zeros((2 * OWN, OWN), F32))
    upper, lower = table[:OWN].T[:HEADS], table[OWN:].T[:HEADS]
    left_lanes = lax.broadcasted_iota(jnp.int32, (HEADS, OWN), 1) < HALF
    zmine[pl.ds(0, HEADS)] = jnp.where(left_lanes, upper, pltpu.roll(lower, HALF, 1))
    zmine[pl.ds(HEADS, HEADS)] = jnp.where(left_lanes, pltpu.roll(upper, HALF, 1), lower)
    for dr, dc in AROUND:

        @pl.when(has(dr, dc))
        def _():
            z_copy(dr, dc).start()

    def key_b(p, carry):
        for n in (0, 1):
            fb[p, n] = jnp.exp(dot_nt(km[p, pl.ds(OWN * n, OWN)], qb[n, p])) * mask_b[n]
        return carry

    lax.fori_loop(0, PAIRS, key_b, 0)

    def by_heads(array):
        parts = [array[HALF * i : HALF * (i + 1)] for i in range(4)]
        return jnp.concatenate(
            [jnp.where(first_lanes, parts[2 * n], parts[2 * n + 1]) for n in (0, 1)], axis=0
        )

    def query_second(p, carry):
        inverse, delta = zbc[p], dbc[p]
        wide = jnp.concatenate([inverse] * 3, axis=1)
        dscore = ea[p] * wide * (pa[p] - jnp.concatenate([delta] * 3, axis=1))
        result = dot(dscore.astype(BF16), ka[p])
        more = []
        for n in (0, 1):
            rows = slice(OWN * n, OWN * (n + 1))
            i2 = jnp.concatenate([inverse[rows], inverse[rows, :HALF]], axis=1)
            d2 = jnp.concatenate([delta[rows], delta[rows, :HALF]], axis=1)
            dscore = eb[p, n] * i2 * (pb[p, n] - d2)
            more.append(dot(dscore.astype(BF16), kb[n, p]))
        dqkv[0, p] = by_heads(result + jnp.concatenate(more, axis=0))
        return carry

    lax.fori_loop(0, PAIRS, query_second, 0)
    ones128 = head_ones(PAIR)

    def through_norm(kind):
        blocks = []
        for p in range(PAIRS):
            grads = dqkv[kind, p]
            cols = pl.ds(PAIR * p, PAIR)
            along = head_sums(grads * raws[kind, :, cols], ones128)
            blocks.append(
                (back_own[kind, :, cols] * grads - back_raw[kind, :, cols] * along).astype(BF16)
            )
        return jnp.concatenate(blocks, axis=1)

    partial[...] = dot_nt(through_norm(0), w[:, pl.ds(0, WIDTH)])

    corners(1)

    def key_b_cot(p, carry):
        for n in (0, 1):
            gb[p, n] = dot_nt(vm[p, pl.ds(OWN * n, OWN)], db[n, :, lanes_of(p)])
        return carry

    lax.fori_loop(0, PAIRS, key_b_cot, 0)

    for dr, dc in AROUND:

        @pl.when(has(dr, dc))
        def _():
            z_copy(-dr, -dc).wait_recv()

    znear[slot_of(0, 0)] = zmine[...]
    near_lanes = lax.broadcasted_iota(jnp.int32, (2 * HEADS, OWN), 1) < HALF
    for b, dc in enumerate((0, -1, 1)):
        za[:, pl.ds(b * OWN, OWN)] = znear[slot_of(0, dc)]
    own_up, left_up, right_up = (znear[slot_of(-1, dc)] for dc in (0, -1, 1))
    zb[0, :, pl.ds(0, OWN)] = jnp.where(near_lanes, pltpu.roll(own_up, HALF, 1), left_up)
    zb[0, :, pl.ds(OWN, HALF)] = pltpu.roll(right_up, HALF, 1)[:, :HALF]
    own_down, left_down, right_down = (znear[slot_of(1, dc)] for dc in (0, -1, 1))
    zb[1, :, pl.ds(0, OWN)] = jnp.where(near_lanes, own_down, pltpu.roll(left_down, HALF, 1))
    zb[1, :, pl.ds(OWN, HALF)] = right_down[:, :HALF]

    def terms(e, dp, table, p, halves):
        probs, dscore = [], []
        for i in range(2 * halves):
            rows = slice(HALF * i, HALF * (i + 1))
            first = HEADS * (i % 2)
            prob = e[rows] * table[pl.ds(first + p, 1), :]
            probs.append(prob.astype(BF16))
            dscore.append((prob * (dp[rows] - table[pl.ds(first + PAIRS + p, 1), :])).astype(BF16))
        return jnp.concatenate(probs, axis=0), jnp.concatenate(dscore, axis=0)

    def key_second(p, carry):
        probs, dscore = terms(fa[p], ga[p], za, p, 2)
        dkey = dot(dscore, qa[p])
        dvalue = dot(probs, da[:, :, lanes_of(p)].reshape(GROUP, PAIR))
        more_k, more_v = [], []
        for n in (0, 1):
            probs, dscore = terms(fb[p, n], gb[p, n], zb.at[n], p, 1)
            more_k.append(dot(dscore, qb[n, p]))
            more_v.append(dot(probs, db[n, :, lanes_of(p)]))
        dqkv[1, p] = by_heads(dkey + jnp.concatenate(more_k, axis=0))
        dqkv[2, p] = by_heads(dvalue + jnp.concatenate(more_v, axis=0))
        return carry

    lax.fori_loop(0, PAIRS, key_second, 0)

    dvalues = jnp.concatenate([dqkv[2, p].astype(BF16) for p in range(PAIRS)], axis=1)
    total = partial[...] + dot_nt(dvalues, w[:, pl.ds(2 * WIDTH, WIDTH)])
    total = total + dot_nt(through_norm(1), w[:, pl.ds(WIDTH, WIDTH)])
    out_ref[...] = total.astype(BF16)

    for kind in (0, 1):
        for dr in (-1, 1):

            @pl.when(has(dr, 0))
            def _():
                y_copy(kind, dr).wait_send()

        for dc in (-1, 1):

            @pl.when(has(0, dc))
            def _():
                c_copy(kind, dc).wait_send()

            for n in (0, 1):

                @pl.when(jnp.logical_and(halo_from(n), has(0, dc)))
                def _():
                    f_copy(kind, n, dc).wait_send()

    for dr, dc in AROUND:

        @pl.when(has(dr, dc))
        def _():
            z_copy(dr, dc).wait_send()


def per_device(grid_input, w_qkv, out_weight, head_scale, cotangent):
    dma = pltpu.SemaphoreType.DMA
    masked = pltpu.VMEM((PAIRS, 2 * OWN, PAIR), BF16)
    by_pair = pltpu.VMEM((PAIRS, GROUP, PAIR), BF16)
    halo_by_pair = pltpu.VMEM((2, PAIRS, 3 * HALF, PAIR), BF16)
    scores = pltpu.VMEM((PAIRS, 2 * OWN, GROUP), F32)
    halo_scores = pltpu.VMEM((PAIRS, 2, OWN, 3 * HALF), F32)
    by_query = pltpu.VMEM((PAIRS, 2 * OWN, OWN), F32)
    hbm = pl.BlockSpec(memory_space=pltpu.HBM)
    result = pl.pallas_call(
        kernel,
        out_shape=jax.ShapeDtypeStruct((OWN, D), BF16),
        in_specs=[hbm] * 5,
        out_specs=pl.BlockSpec(memory_space=pltpu.VMEM),
        scratch_shapes=[
            pltpu.SMEM((HEADS,), F32),
            pltpu.VMEM((3, OWN, D), BF16),
            pltpu.VMEM((3, OWN, D), BF16),
            pltpu.VMEM((3, OWN, WIDTH), BF16),
            pltpu.VMEM((2, 3 * HALF, WIDTH), BF16),
            pltpu.VMEM((D, 3 * WIDTH), BF16),
            pltpu.VMEM((D, WIDTH), BF16),
            pltpu.VMEM((OWN, D), BF16),
            *[by_pair] * 3,
            *[halo_by_pair] * 3,
            *[masked] * 4,
            *[pltpu.VMEM((2, OWN, WIDTH), F32)] * 3,
            pltpu.VMEM((2 * OWN, GROUP), F32),
            pltpu.VMEM((2, OWN, 3 * HALF), F32),
            *[scores] * 2,
            *[halo_scores] * 2,
            *[scores] * 2,
            *[halo_scores] * 2,
            *[by_query] * 4,
            pltpu.VMEM((2 * HEADS, OWN), F32),
            pltpu.VMEM((9, 2 * HEADS, OWN), F32),
            pltpu.VMEM((2 * HEADS, GROUP), F32),
            pltpu.VMEM((2, 2 * HEADS, 3 * HALF), F32),
            pltpu.VMEM((3, PAIRS, OWN, PAIR), F32),
            pltpu.VMEM((OWN, D), F32),
            dma((5,)),
            dma((4,)),
            dma((4,)),
            dma((4,)),
            dma((4,)),
            dma((8,)),
            dma((8,)),
            dma((9,)),
            dma((9,)),
        ],
        compiler_params=pltpu.CompilerParams(
            collective_id=0, has_side_effects=True, vmem_limit_bytes=60 << 20
        ),
    )(
        head_scale,
        grid_input.reshape(OWN, D),
        w_qkv,
        out_weight,
        cotangent.reshape(OWN, D),
    )
    return result.reshape(TILE_H, TILE_W, D)


def solution(mesh):
    placed = (P("row", "col", None), P(), P(), P(), P("row", "col", None))
    return jax.shard_map(
        per_device, mesh=mesh, in_specs=placed, out_specs=P("row", "col", None), check_vma=False
    )
```

time: 63.9 us -> 52 us (0.81)
  the two profiles are of different devices: /device:TPU:455 before, /device:TPU:240 now
where the time goes in v2:
time: 52 us; the launch traced here: 51.9 us
  Pallas kernels  50.2 us (97%)
  local copies, waits for them, and re-layouts  1.67 us (3%)
    pallas_call x1, Pallas kernels, per_device(): pl.pallas_call(kernel, out_shape=jax.ShapeDtypeStruct((OWN, D), BF16), in...  50.2 us
    unnamed x1, local copies, waits for them, and re-layouts  1.67 us

profile of v2, /device:TPU:240, one launch (start us, length us, event | category | flops | bytes accessed | tf_op | source)
XLA Modules:
  0.0 51.9 jit_solution(14331697377710490447)
XLA Ops:
  0.0 50.2 %shard_map.55 = bf16[128,1024]{1,0:T(8,128)(2,1)} custom-call(f32[8]{0:T(128)} %scale_hbm.1, bf16[128,1024]{1,0:T(8,128)(2,1)} %bitcast.4, bf16[1024,1536]{1,0:T(8,128)(2,1)} %w_hbm.1, bf16[1024,512]{1,0:T(8,128)(2,1)} %ow_hbm.1, bf16[128,1024]{1,0:T(8,128)(2,1)} %bitcast.5), custom_call_target="tpu_custom_call" | custom-call | tf_op jit(solution)/shard_map/pallas_call | solution.py:502
  50.2 1.7 %copy.7 = bf16[16,8,1024]{2,1,0:T(8,128)(2,1)} copy(bf16[16,8,1024]{2,1,0:T(8,128)(2,1)} %bitcast.3) | data formatting | bytes 524288

commit v3 on v2

--- a/solution.py
+++ b/solution.py
@@ -49,9 +49,9 @@
     scale_ref, xa, xb, da, db, w, ow, cot,
     qa, ka, va, qb, kb, vb,
     qm, km, vm, dm, raws, back_own, back_raw,
-    mask_a, mask_b,
-    ea, pa, eb, pb, fa, ga, fb, gb,
-    zpart, apart, zbc, dbc, zmine, znear, za, zb,
+    mask_a, mask_c, mask_s,
+    ea, pa, fa, ga, ec, pc, fc, gc, es, ps, fsd, gs,
+    zpart, apart, zbc, dbc, zmine, znear, za, zc, zside,
     dqkv, partial,
     local_sem, ys, yr, cs, cr, fs, fr, zs, zr,
 ):
@@ -201,12 +201,12 @@
     quad_rows = [scale_row(0, 4), scale_row(4, 4)]
     ones256 = head_ones(256)
 
-    def window(rows, first_half, lanes, block, halo):
+    def window(rows, first_half, lanes, block, halo, first_block):
         row = lax.broadcasted_iota(jnp.int32, (rows, lanes), 0)
         lane = lax.broadcasted_iota(jnp.int32, (rows, lanes), 1)
         own_i = (row // OWN + first_half) * RADIUS + (row % HALF) // TILE_W
         own_j = row % TILE_W
-        b = lane // block
+        b = lane // block + first_block
         there_i = (lane % block) // TILE_W
         if halo:
             there_i = there_i - RADIUS if first_half == 0 else there_i + TILE_H
@@ -216,12 +216,13 @@
         inside = (row_at >= 0) & (row_at < nrow * TILE_H) & (col_at >= 0) & (col_at < ncol * TILE_W)
         return jnp.where(near & inside, 1.0, 0.0)
 
-    mask_a[...] = window(2 * OWN, 0, GROUP, OWN, False)
+    mask_a[...] = window(2 * OWN, 0, GROUP, OWN, False, 0)
     for n in (0, 1):
-        mask_b[n] = window(OWN, n, 3 * HALF, HALF, True)
-
-    def project(x_rows, store, own=False):
-        for n in range(6):
+        mask_c[n] = window(OWN, n, HALF, HALF, True, 0)
+        mask_s[n] = window(OWN, n, OWN, HALF, True, 1)
+
+    def project(x_rows, store, own=False, chunks=range(6)):
+        for n in chunks:
             values = dot(x_rows, w[:, pl.ds(256 * n, 256)])
             kind, quad = n // 2, n % 2
             if kind < 2:
@@ -287,7 +288,7 @@
         apart[p] = tiles(e * dp)
         return carry
 
-    lax.fori_loop(0, PAIRS, query_a, 0)
+    lax.fori_loop(0, PAIRS, query_a, 0, unroll=True)
 
     def pass_on(kind):
         for n, dr in ((0, 1), (1, -1)):
@@ -309,43 +310,67 @@
                 def _():
                     f_copy(kind, n, dc).wait_recv()
 
+    def lanes_of(p):
+        return pl.ds(pl.multiple_of(p * PAIR, PAIR), PAIR)
+
+    NEAR, SIDE = pl.ds(0, HALF), pl.ds(HALF, OWN)
+
+    def rows_of(n):
+        return pl.ds(OWN * n, OWN)
+
+    def each_pair(body):
+        lax.fori_loop(0, PAIRS, body, 0, unroll=True)
+
     pass_on(0)
     project(xb[0], store_b(0))
 
+    def near_scores(p, carry):
+        z, along = [], []
+        for n in (0, 1):
+            e = jnp.exp(dot_nt(qm[p, rows_of(n)], kb[n, p, NEAR])) * mask_c[n]
+            dp = dot_nt(dm[p, rows_of(n)], vb[n, p, NEAR])
+            ec[p, n] = e
+            pc[p, n] = dp
+            fc[p, n] = jnp.exp(dot_nt(km[p, rows_of(n)], qb[n, p, NEAR])) * mask_c[n]
+            z.append(e)
+            along.append(e * dp)
+        zpart[p, :, NEAR] = zpart[p, :, NEAR] + jnp.concatenate(z, axis=0)
+        apart[p, :, NEAR] = apart[p, :, NEAR] + jnp.concatenate(along, axis=0)
+        return carry
+
+    each_pair(near_scores)
+
     for dc in (-1, 1):
 
         @pl.when(has(0, -dc))
         def _():
             c_copy(1, dc).wait_recv()
-
-    def lanes_of(p):
-        return pl.ds(pl.multiple_of(p * PAIR, PAIR), PAIR)
 
     def key_a(p, carry):
         fa[p] = jnp.exp(dot_nt(km[p], qa[p])) * mask_a[...]
         ga[p] = dot_nt(vm[p], da[:, :, lanes_of(p)].reshape(GROUP, PAIR))
         return carry
 
-    lax.fori_loop(0, PAIRS, key_a, 0)
-
+    each_pair(key_a)
+
+    pass_on(1)
     corners(0)
-    project(xb[1:3].reshape(2 * OWN, D), store_b(1))
-    pass_on(1)
+    x_sides = xb[1:3].reshape(2 * OWN, D)
+    project(x_sides, store_b(1), chunks=range(2, 6))
 
     lane = lax.broadcasted_iota(jnp.int32, (2 * OWN, OWN), 1)
 
-    def query_b(p, table):
+    def side_scores(p, table):
         z, along = [], []
         for n in (0, 1):
-            rows = pl.ds(OWN * n, OWN)
-            e = jnp.exp(dot_nt(qm[p, rows], kb[n, p])) * mask_b[n]
-            dp = dot_nt(dm[p, rows], vb[n, p])
-            eb[p, n] = e
-            pb[p, n] = dp
-            z.append(jnp.sum(e, axis=1, keepdims=True))
-            along.append(jnp.sum(e * dp, axis=1, keepdims=True))
-        z = jnp.concatenate(z, axis=0) + jnp.sum(zpart[p], axis=1, keepdims=True)
-        along = jnp.concatenate(along, axis=0) + jnp.sum(apart[p], axis=1, keepdims=True)
+            e = jnp.exp(dot_nt(qm[p, rows_of(n)], kb[n, p, SIDE])) * mask_s[n]
+            dp = dot_nt(dm[p, rows_of(n)], vb[n, p, SIDE])
+            es[p, n] = e
+            ps[p, n] = dp
+            z.append(e)
+            along.append(e * dp)
+        z = jnp.sum(jnp.concatenate(z, axis=0) + zpart[p], axis=1, keepdims=True)
+        along = jnp.sum(jnp.concatenate(along, axis=0) + apart[p], axis=1, keepdims=True)
         inverse = 1.0 / z
         delta = along * inverse
         zbc[p] = jnp.broadcast_to(inverse, (2 * OWN, OWN))
@@ -353,7 +378,7 @@
         table = jnp.where(lane == p, inverse, table)
         return jnp.where(lane == PAIRS + p, delta, table)
 
-    table = lax.fori_loop(0, PAIRS, query_b, jnp.zeros((2 * OWN, OWN), F32))
+    table = lax.fori_loop(0, PAIRS, side_scores, jnp.zeros((2 * OWN, OWN), F32), unroll=True)
     upper, lower = table[:OWN].T[:HEADS], table[OWN:].T[:HEADS]
     left_lanes = lax.broadcasted_iota(jnp.int32, (HEADS, OWN), 1) < HALF
     zmine[pl.ds(0, HEADS)] = jnp.where(left_lanes, upper, pltpu.roll(lower, HALF, 1))
@@ -364,12 +389,15 @@
         def _():
             z_copy(dr, dc).start()
 
-    def key_b(p, carry):
-        for n in (0, 1):
-            fb[p, n] = jnp.exp(dot_nt(km[p, pl.ds(OWN * n, OWN)], qb[n, p])) * mask_b[n]
-        return carry
-
-    lax.fori_loop(0, PAIRS, key_b, 0)
+
+    project(x_sides, store_b(1), chunks=range(2))
+
+    def key_sides(p, carry):
+        for n in (0, 1):
+            fsd[p, n] = jnp.exp(dot_nt(km[p, rows_of(n)], qb[n, p, SIDE])) * mask_s[n]
+        return carry
+
+    each_pair(key_sides)
 
     def by_heads(array):
         parts = [array[HALF * i : HALF * (i + 1)] for i in range(4)]
@@ -385,14 +413,14 @@
         more = []
         for n in (0, 1):
             rows = slice(OWN * n, OWN * (n + 1))
-            i2 = jnp.concatenate([inverse[rows], inverse[rows, :HALF]], axis=1)
-            d2 = jnp.concatenate([delta[rows], delta[rows, :HALF]], axis=1)
-            dscore = eb[p, n] * i2 * (pb[p, n] - d2)
-            more.append(dot(dscore.astype(BF16), kb[n, p]))
+            dscore = ec[p, n] * inverse[rows, :HALF] * (pc[p, n] - delta[rows, :HALF])
+            near = dot(dscore.astype(BF16), kb[n, p, NEAR])
+            dscore = es[p, n] * inverse[rows] * (ps[p, n] - delta[rows])
+            more.append(near + dot(dscore.astype(BF16), kb[n, p, SIDE]))
         dqkv[0, p] = by_heads(result + jnp.concatenate(more, axis=0))
         return carry
 
-    lax.fori_loop(0, PAIRS, query_second, 0)
+    each_pair(query_second)
     ones128 = head_ones(PAIR)
 
     def through_norm(kind):
@@ -410,12 +438,13 @@
 
     corners(1)
 
-    def key_b_cot(p, carry):
-        for n in (0, 1):
-            gb[p, n] = dot_nt(vm[p, pl.ds(OWN * n, OWN)], db[n, :, lanes_of(p)])
-        return carry
-
-    lax.fori_loop(0, PAIRS, key_b_cot, 0)
+    def key_halo_cot(p, carry):
+        for n in (0, 1):
+            gc[p, n] = dot_nt(vm[p, rows_of(n)], db[n, NEAR, lanes_of(p)])
+            gs[p, n] = dot_nt(vm[p, rows_of(n)], db[n, SIDE, lanes_of(p)])
+        return carry
+
+    each_pair(key_halo_cot)
 
     for dr, dc in AROUND:
 
@@ -428,11 +457,11 @@
     for b, dc in enumerate((0, -1, 1)):
         za[:, pl.ds(b * OWN, OWN)] = znear[slot_of(0, dc)]
     own_up, left_up, right_up = (znear[slot_of(-1, dc)] for dc in (0, -1, 1))
-    zb[0, :, pl.ds(0, OWN)] = jnp.where(near_lanes, pltpu.roll(own_up, HALF, 1), left_up)
-    zb[0, :, pl.ds(OWN, HALF)] = pltpu.roll(right_up, HALF, 1)[:, :HALF]
+    zc[0] = pltpu.roll(own_up, HALF, 1)[:, :HALF]
+    zside[0] = jnp.where(near_lanes, pltpu.roll(left_up, HALF, 1), right_up)
     own_down, left_down, right_down = (znear[slot_of(1, dc)] for dc in (0, -1, 1))
-    zb[1, :, pl.ds(0, OWN)] = jnp.where(near_lanes, own_down, pltpu.roll(left_down, HALF, 1))
-    zb[1, :, pl.ds(OWN, HALF)] = right_down[:, :HALF]
+    zc[1] = own_down[:, :HALF]
+    zside[1] = jnp.where(near_lanes, left_down, pltpu.roll(right_down, HALF, 1))
 
     def terms(e, dp, table, p, halves):
         probs, dscore = [], []
@@ -450,14 +479,17 @@
         dvalue = dot(probs, da[:, :, lanes_of(p)].reshape(GROUP, PAIR))
         more_k, more_v = [], []
         for n in (0, 1):
-            probs, dscore = terms(fb[p, n], gb[p, n], zb.at[n], p, 1)
-            more_k.append(dot(dscore, qb[n, p]))
-            more_v.append(dot(probs, db[n, :, lanes_of(p)]))
+            probs, dscore = terms(fc[p, n], gc[p, n], zc.at[n], p, 1)
+            near_k = dot(dscore, qb[n, p, NEAR])
+            near_v = dot(probs, db[n, NEAR, lanes_of(p)])
+            probs, dscore = terms(fsd[p, n], gs[p, n], zside.at[n], p, 1)
+            more_k.append(near_k + dot(dscore, qb[n, p, SIDE]))
+            more_v.append(near_v + dot(probs, db[n, SIDE, lanes_of(p)]))
         dqkv[1, p] = by_heads(dkey + jnp.concatenate(more_k, axis=0))
         dqkv[2, p] = by_heads(dvalue + jnp.concatenate(more_v, axis=0))
         return carry
 
-    lax.fori_loop(0, PAIRS, key_second, 0)
+    each_pair(key_second)
 
     dvalues = jnp.concatenate([dqkv[2, p].astype(BF16) for p in range(PAIRS)], axis=1)
     total = partial[...] + dot_nt(dvalues, w[:, pl.ds(2 * WIDTH, WIDTH)])
@@ -496,7 +528,8 @@
     by_pair = pltpu.VMEM((PAIRS, GROUP, PAIR), BF16)
     halo_by_pair = pltpu.VMEM((2, PAIRS, 3 * HALF, PAIR), BF16)
     scores = pltpu.VMEM((PAIRS, 2 * OWN, GROUP), F32)
-    halo_scores = pltpu.VMEM((PAIRS, 2, OWN, 3 * HALF), F32)
+    near_scores = pltpu.VMEM((PAIRS, 2, OWN, HALF), F32)
+    side_scores = pltpu.VMEM((PAIRS, 2, OWN, OWN), F32)
     by_query = pltpu.VMEM((PAIRS, 2 * OWN, OWN), F32)
     hbm = pl.BlockSpec(memory_space=pltpu.HBM)
     result = pl.pallas_call(
@@ -518,16 +551,17 @@
             *[masked] * 4,
             *[pltpu.VMEM((2, OWN, WIDTH), F32)] * 3,
             pltpu.VMEM((2 * OWN, GROUP), F32),
-            pltpu.VMEM((2, OWN, 3 * HALF), F32),
-            *[scores] * 2,
-            *[halo_scores] * 2,
-            *[scores] * 2,
-            *[halo_scores] * 2,
+            pltpu.VMEM((2, OWN, HALF), F32),
+            pltpu.VMEM((2, OWN, OWN), F32),
+            *[scores] * 4,
+            *[near_scores] * 4,
+            *[side_scores] * 4,
             *[by_query] * 4,
             pltpu.VMEM((2 * HEADS, OWN), F32),
             pltpu.VMEM((9, 2 * HEADS, OWN), F32),
             pltpu.VMEM((2 * HEADS, GROUP), F32),
-            pltpu.VMEM((2, 2 * HEADS, 3 * HALF), F32),
+            pltpu.VMEM((2, 2 * HEADS, HALF), F32),
+            pltpu.VMEM((2, 2 * HEADS, OWN), F32),
             pltpu.VMEM((3, PAIRS, OWN, PAIR), F32),
             pltpu.VMEM((OWN, D), F32),
             dma((5,)),

time: 52 us -> 49.4 us (0.950)
  Pallas kernels: 50.2 us -> 47.6 us
    pallas_call x1, Pallas kernels: 50.2 us -> 47.6 us  [per_device(): pl.pallas_call(kernel, out_shape=jax.ShapeDtypeStruct((OWN, D), BF16), in...]
where the time goes in v3:
time: 49.4 us; the launch traced here: 49.3 us
  Pallas kernels  47.6 us (96%)
  local copies, waits for them, and re-layouts  1.67 us (3%)
    pallas_call x1, Pallas kernels, per_device(): pl.pallas_call(kernel, out_shape=jax.ShapeDtypeStruct((OWN, D), BF16), in...  47.6 us
    unnamed x1, local copies, waits for them, and re-layouts  1.67 us

profile of v3, /device:TPU:240, one launch (start us, length us, event | category | flops | bytes accessed | tf_op | source)
XLA Modules:
  0.0 49.3 jit_solution(9260651783524240304)
XLA Ops:
  0.0 47.6 %shard_map.55 = bf16[128,1024]{1,0:T(8,128)(2,1)} custom-call(f32[8]{0:T(128)} %scale_hbm.1, bf16[128,1024]{1,0:T(8,128)(2,1)} %bitcast.4, bf16[1024,1536]{1,0:T(8,128)(2,1)} %w_hbm.1, bf16[1024,512]{1,0:T(8,128)(2,1)} %ow_hbm.1, bf16[128,1024]{1,0:T(8,128)(2,1)} %bitcast.5), custom_call_target="tpu_custom_call" | custom-call | tf_op jit(solution)/shard_map/pallas_call | solution.py:535
  47.6 1.7 %copy.7 = bf16[16,8,1024]{2,1,0:T(8,128)(2,1)} copy(bf16[16,8,1024]{2,1,0:T(8,128)(2,1)} %bitcast.3) | data formatting | bytes 524288

commit v4 on v3

--- a/solution.py
+++ b/solution.py
@@ -15,6 +15,7 @@
 TILE_H = 16
 TILE_W = 8
 OWN = TILE_H * TILE_W
+RUN = 8
 HALF = OWN // 2
 GROUP = 3 * OWN
 
@@ -52,8 +53,8 @@
     mask_a, mask_c, mask_s,
     ea, pa, fa, ga, ec, pc, fc, gc, es, ps, fsd, gs,
     zpart, apart, zbc, dbc, zmine, znear, za, zc, zside,
-    dqkv, partial,
-    local_sem, ys, yr, cs, cr, fs, fr, zs, zr,
+    dqkv, partial, xrelay, drelay,
+    local_sem, ys, yr, cs, cr, fs, fr, zs, zr, rs, rr,
 ):
     nrow, ncol = lax.axis_size("row"), lax.axis_size("col")
     r, c = lax.axis_index("row"), lax.axis_index("col")
@@ -75,6 +76,17 @@
             device_id=device(dr, dc), device_id_type=MESH,
         )
 
+    place = lax.rem(c, RUN)
+    crosses = {
+        1: jnp.logical_and(place == RUN - 1, c < ncol - 1),
+        -1: jnp.logical_and(place == 0, c > 0),
+    }
+    relays = {
+        1: jnp.logical_and(place == 1, c < ncol - RUN),
+        -1: jnp.logical_and(place == RUN - 2, c >= RUN),
+    }
+    TO_RELAY, FROM_RELAY = -(RUN - 2), RUN - 1
+
     barrier = pltpu.get_barrier_semaphore()
     count = 0
     for dr, dc in AROUND:
@@ -84,6 +96,14 @@
         @pl.when(there)
         def _():
             pl.semaphore_signal(barrier, inc=1, device_id=device(dr, dc), device_id_type=MESH)
+
+    for dc in (-1, 1):
+        count = count + crosses[dc].astype(jnp.int32) + relays[dc].astype(jnp.int32)
+        for here, to in ((relays[dc], -TO_RELAY * dc), (crosses[-dc], -FROM_RELAY * dc)):
+
+            @pl.when(here)
+            def _():
+                pl.semaphore_signal(barrier, inc=1, device_id=device(0, to), device_id_type=MESH)
 
     local = [
         pltpu.make_async_copy(src, dst, local_sem.at[i])
@@ -111,6 +131,34 @@
         i = 2 * kind + (dc > 0)
         return remote(src, dst.at[block_of(-dc)], cs.at[i], cr.at[i], 0, dc)
 
+    def to_relay(kind, dc):
+        src, dst = (x_hbm, xrelay) if kind == 0 else (da.at[0], drelay)
+        return remote(src, dst, cs.at[2 * kind + (dc > 0)], rr.at[kind], 0, TO_RELAY * dc)
+
+    def from_relay(kind, dc):
+        src, dst = (xrelay, xa) if kind == 0 else (drelay, da)
+        i = 2 * kind + (dc > 0)
+        return remote(src, dst.at[block_of(-dc)], rs.at[kind], cr.at[i], 0, FROM_RELAY * dc)
+
+    def send_own(kind):
+        for dc in (-1, 1):
+
+            @pl.when(jnp.logical_and(has(0, dc), jnp.logical_not(crosses[dc])))
+            def _():
+                c_copy(kind, dc).start()
+
+            @pl.when(crosses[dc])
+            def _():
+                to_relay(kind, dc).start()
+
+    def relay(kind):
+        for dc in (-1, 1):
+
+            @pl.when(relays[dc])
+            def _():
+                to_relay(kind, dc).wait_recv()
+                from_relay(kind, dc).start()
+
     def f_copy(kind, n, dc):
         i = 4 * kind + 2 * n + (dc > 0)
         b = block_of(-dc)
@@ -134,11 +182,7 @@
         def _():
             y_copy(0, dr).start()
 
-    for dc in (-1, 1):
-
-        @pl.when(has(0, dc))
-        def _():
-            c_copy(0, dc).start()
+    send_own(0)
 
     for dc in (-1, 1):
 
@@ -176,11 +220,7 @@
         def _():
             y_copy(1, dr).start()
 
-    for dc in (-1, 1):
-
-        @pl.when(has(0, dc))
-        def _():
-            c_copy(1, dc).start()
+    send_own(1)
 
     local[4].wait()
     local[2].wait()
@@ -220,6 +260,8 @@
     for n in (0, 1):
         mask_c[n] = window(OWN, n, HALF, HALF, True, 0)
         mask_s[n] = window(OWN, n, OWN, HALF, True, 1)
+
+    relay(0)
 
     def project(x_rows, store, own=False, chunks=range(6)):
         for n in chunks:
@@ -268,28 +310,6 @@
                 to[p, half(2 * n)] = jnp.where(first_lanes, rows, zero)
                 to[p, half(2 * n + 1)] = jnp.where(first_lanes, zero, rows)
 
-    for dc in (-1, 1):
-
-        @pl.when(has(0, -dc))
-        def _():
-            c_copy(0, dc).wait_recv()
-
-    project(xa[1:3].reshape(2 * OWN, D), store_a(OWN))
-
-    def tiles(array):
-        return array[:, :OWN] + array[:, OWN : 2 * OWN] + array[:, 2 * OWN :]
-
-    def query_a(p, carry):
-        e = jnp.exp(dot_nt(qm[p], ka[p])) * mask_a[...]
-        dp = dot_nt(dm[p], va[p])
-        ea[p] = e
-        pa[p] = dp
-        zpart[p] = tiles(e)
-        apart[p] = tiles(e * dp)
-        return carry
-
-    lax.fori_loop(0, PAIRS, query_a, 0, unroll=True)
-
     def pass_on(kind):
         for n, dr in ((0, 1), (1, -1)):
 
@@ -334,24 +354,35 @@
             fc[p, n] = jnp.exp(dot_nt(km[p, rows_of(n)], qb[n, p, NEAR])) * mask_c[n]
             z.append(e)
             along.append(e * dp)
-        zpart[p, :, NEAR] = zpart[p, :, NEAR] + jnp.concatenate(z, axis=0)
-        apart[p, :, NEAR] = apart[p, :, NEAR] + jnp.concatenate(along, axis=0)
+        rest = jnp.zeros((2 * OWN, HALF), F32)
+        zpart[p] = jnp.concatenate([jnp.concatenate(z, axis=0), rest], axis=1)
+        apart[p] = jnp.concatenate([jnp.concatenate(along, axis=0), rest], axis=1)
         return carry
 
     each_pair(near_scores)
 
+    relay(1)
     for dc in (-1, 1):
 
         @pl.when(has(0, -dc))
         def _():
-            c_copy(1, dc).wait_recv()
-
-    def key_a(p, carry):
-        fa[p] = jnp.exp(dot_nt(km[p], qa[p])) * mask_a[...]
-        ga[p] = dot_nt(vm[p], da[:, :, lanes_of(p)].reshape(GROUP, PAIR))
+            c_copy(0, dc).wait_recv()
+
+    project(xa[1:3].reshape(2 * OWN, D), store_a(OWN))
+
+    def tiles(array):
+        return array[:, :OWN] + array[:, OWN : 2 * OWN] + array[:, 2 * OWN :]
+
+    def query_a(p, carry):
+        e = jnp.exp(dot_nt(qm[p], ka[p])) * mask_a[...]
+        dp = dot_nt(dm[p], va[p])
+        ea[p] = e
+        pa[p] = dp
+        zpart[p] = zpart[p] + tiles(e)
+        apart[p] = apart[p] + tiles(e * dp)
         return carry
 
-    each_pair(key_a)
+    lax.fori_loop(0, PAIRS, query_a, 0, unroll=True)
 
     pass_on(1)
     corners(0)
@@ -399,6 +430,19 @@
 
     each_pair(key_sides)
 
+    for dc in (-1, 1):
+
+        @pl.when(has(0, -dc))
+        def _():
+            c_copy(1, dc).wait_recv()
+
+    def key_a(p, carry):
+        fa[p] = jnp.exp(dot_nt(km[p], qa[p])) * mask_a[...]
+        ga[p] = dot_nt(vm[p], da[:, :, lanes_of(p)].reshape(GROUP, PAIR))
+        return carry
+
+    each_pair(key_a)
+
     def by_heads(array):
         parts = [array[HALF * i : HALF * (i + 1)] for i in range(4)]
         return jnp.concatenate(
@@ -508,6 +552,10 @@
             @pl.when(has(0, dc))
             def _():
                 c_copy(kind, dc).wait_send()
+
+            @pl.when(relays[dc])
+            def _():
+                from_relay(kind, dc).wait_send()
 
             for n in (0, 1):
 
@@ -564,6 +612,8 @@
             pltpu.VMEM((2, 2 * HEADS, OWN), F32),
             pltpu.VMEM((3, PAIRS, OWN, PAIR), F32),
             pltpu.VMEM((OWN, D), F32),
+            pltpu.VMEM((OWN, D), BF16),
+            pltpu.VMEM((OWN, WIDTH), BF16),
             dma((5,)),
             dma((4,)),
             dma((4,)),
@@ -573,6 +623,8 @@
             dma((8,)),
             dma((9,)),
             dma((9,)),
+            dma((2,)),
+            dma((2,)),
         ],
         compiler_params=pltpu.CompilerParams(
             collective_id=0, has_side_effects=True, vmem_limit_bytes=60 << 20

time: 49.4 us -> 44.9 us (0.909)
  Pallas kernels: 47.6 us -> 42.8 us
    pallas_call x1, Pallas kernels: 47.6 us -> 42.8 us  [per_device(): pl.pallas_call(kernel, out_shape=jax.ShapeDtypeStruct((OWN, D), BF16), in...]
where the time goes in v4:
time: 44.9 us; the launch traced here: 44.4 us
  Pallas kernels  42.8 us (95%)
  local copies, waits for them, and re-layouts  1.67 us (4%)
    pallas_call x1, Pallas kernels, per_device(): pl.pallas_call(kernel, out_shape=jax.ShapeDtypeStruct((OWN, D), BF16), in...  42.8 us
    unnamed x1, local copies, waits for them, and re-layouts  1.67 us

profile of v4, /device:TPU:240, one launch (start us, length us, event | category | flops | bytes accessed | tf_op | source)
XLA Modules:
  0.0 44.4 jit_solution(388267587133679558)
XLA Ops:
  0.0 42.8 %shard_map.55 = bf16[128,1024]{1,0:T(8,128)(2,1)} custom-call(f32[8]{0:T(128)} %scale_hbm.1, bf16[128,1024]{1,0:T(8,128)(2,1)} %bitcast.4, bf16[1024,1536]{1,0:T(8,128)(2,1)} %w_hbm.1, bf16[1024,512]{1,0:T(8,128)(2,1)} %ow_hbm.1, bf16[128,1024]{1,0:T(8,128)(2,1)} %bitcast.5), custom_call_target="tpu_custom_call" | custom-call | tf_op jit(solution)/shard_map/pallas_call | solution.py:583
  42.8 1.7 %copy.7 = bf16[16,8,1024]{2,1,0:T(8,128)(2,1)} copy(bf16[16,8,1024]{2,1,0:T(8,128)(2,1)} %bitcast.3) | data formatting | bytes 524288

commit v5 on v4

--- a/solution.py
+++ b/solution.py
@@ -214,12 +214,6 @@
     for n in range(2):
         cols = pl.ds(256 * n, 256)
         da[0, :, cols] = dot(cot[...], ow[:, cols]).astype(BF16)
-    for dr in (-1, 1):
-
-        @pl.when(has(dr, 0))
-        def _():
-            y_copy(1, dr).start()
-
     send_own(1)
 
     local[4].wait()
@@ -276,7 +270,7 @@
                     back_own[kind, :, cols] = factor
                     back_raw[kind, :, cols] = factor * values / squares
                 else:
-                    squares = dot((values * values).astype(BF16), ones256) + norm_epsilon
+                    squares = head_sums(values * values, ones256) + norm_epsilon
                     factor = quad_rows[quad] * lax.rsqrt(squares)
                 values = values * factor
             result = values.astype(BF16)
@@ -298,6 +292,12 @@
         return store
 
     project(xa[0], store_a(0), own=True)
+    for dr in (-1, 1):
+
+        @pl.when(has(dr, 0))
+        def _():
+            y_copy(1, dr).start()
+
     first_lanes = lax.broadcasted_iota(jnp.int32, (HALF, PAIR), 1) < HEAD_DIM
     zero = jnp.zeros((HALF, PAIR), BF16)
     for p in range(PAIRS):
@@ -384,7 +384,6 @@
 
     lax.fori_loop(0, PAIRS, query_a, 0, unroll=True)
 
-    pass_on(1)
     corners(0)
     x_sides = xb[1:3].reshape(2 * OWN, D)
     project(x_sides, store_b(1), chunks=range(2, 6))
@@ -420,6 +419,7 @@
         def _():
             z_copy(dr, dc).start()
 
+    pass_on(1)
 
     project(x_sides, store_b(1), chunks=range(2))
 

time: 44.9 us -> 44.4 us (0.989)
  the two profiles are of different devices: /device:TPU:240 before, /device:TPU:249 now
where the time goes in v5:
time: 44.4 us; the launch traced here: 44.3 us
  Pallas kernels  42.6 us (96%)
  local copies, waits for them, and re-layouts  1.67 us (4%)
    pallas_call x1, Pallas kernels, per_device(): pl.pallas_call(kernel, out_shape=jax.ShapeDtypeStruct((OWN, D), BF16), in...  42.6 us
    unnamed x1, local copies, waits for them, and re-layouts  1.67 us

profile of v5, /device:TPU:249, one launch (start us, length us, event | category | flops | bytes accessed | tf_op | source)
XLA Modules:
  0.0 44.3 jit_solution(12364533273366314447)
XLA Ops:
  0.0 42.6 %shard_map.55 = bf16[128,1024]{1,0:T(8,128)(2,1)} custom-call(f32[8]{0:T(128)} %scale_hbm.1, bf16[128,1024]{1,0:T(8,128)(2,1)} %bitcast.4, bf16[1024,1536]{1,0:T(8,128)(2,1)} %w_hbm.1, bf16[1024,512]{1,0:T(8,128)(2,1)} %ow_hbm.1, bf16[128,1024]{1,0:T(8,128)(2,1)} %bitcast.5), custom_call_target="tpu_custom_call" | custom-call | tf_op jit(solution)/shard_map/pallas_call | solution.py:583
  42.6 1.7 %copy.7 = bf16[16,8,1024]{2,1,0:T(8,128)(2,1)} copy(bf16[16,8,1024]{2,1,0:T(8,128)(2,1)} %bitcast.3) | data formatting | bytes 524288

commit v6 on v5

--- a/solution.py
+++ b/solution.py
@@ -176,13 +176,13 @@
         return has(-1, 0) if n == 0 else has(1, 0)
 
     pl.semaphore_wait(barrier, count)
+    send_own(0)
     for dr in (-1, 1):
 
         @pl.when(has(dr, 0))
         def _():
             y_copy(0, dr).start()
 
-    send_own(0)
 
     for dc in (-1, 1):
 

time: 44.4 us -> 44.5 us (level)
  no operation moved by 1% of the time
where the time goes in v6:
time: 44.5 us; the launch traced here: 44.3 us
  Pallas kernels  42.7 us (96%)
  local copies, waits for them, and re-layouts  1.67 us (4%)
    pallas_call x1, Pallas kernels, per_device(): pl.pallas_call(kernel, out_shape=jax.ShapeDtypeStruct((OWN, D), BF16), in...  42.7 us
    unnamed x1, local copies, waits for them, and re-layouts  1.67 us

profile of v6, /device:TPU:249, one launch (start us, length us, event | category | flops | bytes accessed | tf_op | source)
XLA Modules:
  0.0 44.3 jit_solution(9037436748453756238)
XLA Ops:
  0.0 42.7 %shard_map.55 = bf16[128,1024]{1,0:T(8,128)(2,1)} custom-call(f32[8]{0:T(128)} %scale_hbm.1, bf16[128,1024]{1,0:T(8,128)(2,1)} %bitcast.4, bf16[1024,1536]{1,0:T(8,128)(2,1)} %w_hbm.1, bf16[1024,512]{1,0:T(8,128)(2,1)} %ow_hbm.1, bf16[128,1024]{1,0:T(8,128)(2,1)} %bitcast.5), custom_call_target="tpu_custom_call" | custom-call | tf_op jit(solution)/shard_map/pallas_call | solution.py:583
  42.7 1.7 %copy.7 = bf16[16,8,1024]{2,1,0:T(8,128)(2,1)} copy(bf16[16,8,1024]{2,1,0:T(8,128)(2,1)} %bitcast.3) | data formatting | bytes 524288
